TPU v7x, 32 devices: a whole 2x2x4 slice. The times are simulated.
32 devices in a mesh: gx: 4 (over x, core), gy: 8 (over z, y).
Axes of the slice: x: 2, y: 2, z: 4, core: 2. Of those that a mesh axis runs over, the one named last changes fastest.
Arguments:
- leaf_raw: float32 [4, 8, 768, 768], P('gx', 'gy'), may hold values from -32 to 80, as said below
- medium_class: int32 [4, 8, 12], P('gx', 'gy'), may hold values from 0 to 7
- wave_table: float32 [8], replicated, may hold values from 1 to 4
- boundary_data: float32 [4, 8, 384, 128], P('gx', 'gy'), may hold values from -6 to 6
Outputs:
- parent_rows: float32 [4, 8, 384, 1536], P('gx', 'gy')
- interface_values: float32 [4, 8, 384, 128], P('gx', 'gy')
Inputs may be any that keep to these rules, and one draw needn't show every extreme that they name: Each tile's block leaf_raw[p, q] is symmetric positive semidefinite.
All inputs are finite; a program needn't handle non-finite values.
Results may differ from a plain program's by a relative error of at most 0.0001.
Values sent between devices are 32-bit elements; how exact they have to be, the bound alone decides.
No kernel may reach another device: no remote copies, remote signals or barrier semaphores. Data moves between devices by JAX's collectives and lax.ppermute only.
A program may use at most 64 MiB of HBM per device.

v0:
```python
import functools

import jax
import jax.numpy as jnp
from jax import lax
from jax.experimental import pallas as pl
from jax.experimental.pallas import tpu as pltpu
from jax.sharding import PartitionSpec as P

f32 = jnp.float32
bf16 = jnp.bfloat16
VM = pl.BlockSpec(memory_space=pltpu.VMEM)
SM = pl.BlockSpec(memory_space=pltpu.SMEM)
LEAST = 4.0


def shifted(shard, axis):
    size = lax.axis_size(axis)
    return lax.ppermute(shard, axis, [(i, (i + size // 2) % size) for i in range(size)])


def parts_of(x, count=2):
    parts = []
    for _ in range(count - 1):
        parts.append(x.astype(bf16))
        x = x - parts[-1].astype(f32)
    return parts + [x.astype(bf16)]


def dot_of(left, right, contract):
    return lax.dot_general(left, right, (contract, ((), ())), preferred_element_type=f32)


def mul_parts(left, right, contract=((1,), (0,))):
    depth = max(len(left), len(right))
    total = None
    for order in reversed(range(depth)):
        for i in range(order + 1):
            if i < len(left) and order - i < len(right):
                term = dot_of(left[i], right[order - i], contract)
                total = term if total is None else total + term
    return total


def mul(left, right):
    return mul_parts(parts_of(left), parts_of(right))


def mul_t(left, right):
    return mul_parts(parts_of(left), parts_of(right), ((0,), (0,)))


def rows_of(shape):
    return lax.broadcasted_iota(jnp.int32, shape, 0)


def cols_of(shape):
    return lax.broadcasted_iota(jnp.int32, shape, 1)


def eye(n):
    return (rows_of((n, n)) == cols_of((n, n))).astype(f32)


def invert(mat_ref, least, inv_ref, res_ref):
    n = mat_ref.shape[0]
    unit = eye(n)
    mat = mat_ref[...]
    most = jnp.max(jnp.sum(jnp.abs(mat), axis=0, keepdims=True))
    scale = 2.0 / (most + least)
    eps = (most - least) / (most + least)
    res = unit - scale * mat
    gain = 2.0 / (2.0 - eps * eps)
    inv_ref[...] = (gain * scale) * (unit + res)
    res_parts = parts_of(res)
    res_ref[...] = (1.0 - gain) * unit + gain * mul_parts(res_parts, res_parts)

    def fast(carry):
        eps, noise = carry
        gain = 2.0 / (2.0 - eps * eps)
        inv = inv_ref[...]
        res_parts = parts_of(res_ref[...])
        inv_ref[...] = gain * (inv + mul_parts(res_parts, parts_of(inv)))
        res_ref[...] = (1.0 - gain) * unit + gain * mul_parts(res_parts, res_parts)
        return gain * eps * eps * 0.5, 2.0 * gain * eps * noise + 3e-5

    eps, noise = lax.while_loop(
        lambda carry: carry[0] > 0.02, fast, (gain * eps * eps * 0.5, jnp.float32(6e-5))
    )
    mat_parts = parts_of(mat, 3)

    def correct(bound):
        inv = inv_ref[...]
        inv_parts = parts_of(inv, 3)
        res = unit - mul_parts(mat_parts, inv_parts)
        inv_ref[...] = inv + mul_parts(inv_parts[:2], parts_of(res))
        return bound * bound

    lax.while_loop(
        lambda bound: bound > 1e-6,
        correct,
        jnp.minimum(eps + noise + 1e-5 * (most / least), 0.5),
    )


def pack_kernel(class_ref, table_ref, raw_ref, data_ref, one_ref, two_ref, three_ref, rest_ref):
    bound = raw_ref.shape[0]
    side = bound // 4
    blk = bound // class_ref.shape[0]
    shape = (side, side)
    row, col = rows_of(shape), cols_of(shape)

    def with_diagonal(face, start):
        level = jnp.zeros(shape, f32)
        for k in range(side // blk):
            value = LEAST + table_ref[class_ref[start // blk + k]]
            level = jnp.where(row // blk == k, value, level)
        return face + jnp.where(row == col, level, 0.0)

    face = with_diagonal(raw_ref[2 * side : 3 * side, 2 * side : 3 * side], 2 * side)
    inner = with_diagonal(raw_ref[3 * side :, 3 * side :], 3 * side)
    one_ref[:side, :side] = jnp.where(row <= col, inner, face)
    one_ref[:side, side:] = raw_ref[3 * side :, 2 * side : 3 * side]
    one_ref[side:, :] = jnp.zeros((8, 2 * side), f32)
    one_ref[side : side + 1, :side] = jnp.sum(
        jnp.where(row == col, face, 0.0), axis=0, keepdims=True
    )
    inner_out = raw_ref[3 * side :, : 2 * side]
    face_out = raw_ref[2 * side : 3 * side, : 2 * side]
    two_ref[...] = inner_out
    three_ref[...] = face_out
    rest_ref[:side] = inner_out
    rest_ref[side : 2 * side] = face_out
    ncol = data_ref.shape[1]
    for k in range(2 * side // ncol):
        rest_ref[2 * side :, k * ncol : (k + 1) * ncol] = data_ref[k * ncol : (k + 1) * ncol]


def unpack(one_ref):
    side = one_ref.shape[1] // 2
    shape = (side, side)
    row, col = rows_of(shape), cols_of(shape)
    packed = one_ref[:side, :side]
    flipped = packed.T
    inner = jnp.where(row <= col, packed, flipped)
    face = jnp.where(row > col, packed, jnp.where(row < col, flipped, one_ref[side : side + 1, :side]))
    return inner, face, one_ref[:side, side:]


def pair_level(least, own_ref, sib_ref, mat, res, inv_ref, fold_ref):
    side = own_ref.shape[1] // 2
    inner_a, face_a, cross_a = unpack(own_ref)
    inner_b, face_b, cross_b = unpack(sib_ref)
    mat[...] = inner_a + inner_b
    invert(mat, least, inv_ref, res)
    inv_parts = parts_of(inv_ref[...])
    parts_a, parts_b = parts_of(cross_a), parts_of(cross_b)
    fold_a = mul_parts(parts_a, inv_parts, ((0,), (0,)))
    fold_b = mul_parts(parts_b, inv_parts, ((0,), (0,)))
    fold_ref[:side] = fold_a
    fold_ref[side:] = fold_b
    fold_a, fold_b = parts_of(fold_a), parts_of(fold_b)
    aa = face_a - mul_parts(fold_a, parts_a)
    ab = -mul_parts(fold_a, parts_b)
    ba = -mul_parts(fold_b, parts_a)
    bb = face_b - mul_parts(fold_b, parts_b)
    return aa, ab, ba, bb


def least_of(table_ref):
    least = table_ref[0]
    for k in range(1, table_ref.shape[0]):
        least = jnp.minimum(least, table_ref[k])
    return 2.0 * (LEAST + least)


def own_kernel(table_ref, own_ref, sib_ref, inv_ref, fold_ref, face_ref, mat, res):
    side = own_ref.shape[1] // 2
    aa, ab, ba, bb = pair_level(least_of(table_ref), own_ref, sib_ref, mat, res, inv_ref, fold_ref)
    face_ref[:side, :side] = aa
    face_ref[:side, side:] = ab
    face_ref[side:, :side] = ba
    face_ref[side:, side:] = bb


def far_kernel(table_ref, own_ref, sib_ref, near_ref, fold_ref, inv2_ref, mat, res, inv, mat2, res2):
    side = own_ref.shape[1] // 2
    least = least_of(table_ref)
    aa, ab, ba, bb = pair_level(least, own_ref, sib_ref, mat, res, inv, fold_ref)
    mat2[:side, :side] = near_ref[:side, :side] + aa
    mat2[:side, side:] = near_ref[:side, side:] + ab
    mat2[side:, :side] = near_ref[side:, :side] + ba
    mat2[side:, side:] = near_ref[side:, side:] + bb
    invert(mat2, least, inv2_ref, res2)


def rows_kernel(inv_ref, fold_ref, rest_a, rest_b, own_ref, sib_ref, rows_a, rows_b, term_ref, known_ref):
    side = inv_ref.shape[0]
    ncol = term_ref.shape[1]
    fold = parts_of(fold_ref[...])
    term = known = None
    for rest, out, top in ((rest_a, rows_a, 0), (rest_b, rows_b, side)):
        inner_out = parts_of(rest[:side])
        out[...] = -mul_parts(fold, inner_out)
        out[top : top + side] += rest[side : 2 * side]
        data = parts_of(
            jnp.concatenate(
                [rest[2 * side :, k * ncol : (k + 1) * ncol] for k in range(2 * side // ncol)], axis=0
            )
        )
        add = mul_parts(parts_of(out[...]), data)
        more = mul_parts(inner_out, data)
        term = add if term is None else term + add
        known = more if known is None else known + more
    term_ref[...] = term
    known_ref[...] = known


def near_kernel(
    class_ref, table_ref, raw_ref, rest_a, rest_b, inv_ref, inv2_ref, rows_a, rows_b,
    out_a, out_b, scaled_ref,
):
    side = inv_ref.shape[0]
    blk = side * 4 // class_ref.shape[0]
    scaled = mul_t(rows_a[...], inv2_ref[...])
    scaled_ref[...] = scaled
    inner_a = parts_of(rest_a[:side])
    fold = parts_of(mul_parts(inner_a, parts_of(inv_ref[...]), ((0,), (0,))))
    scaled = parts_of(scaled)
    shape = (2 * side, 2 * side)
    row, col = rows_of(shape), cols_of(shape)
    level = jnp.zeros(shape, f32)
    for k in range(2 * side // blk):
        level = jnp.where(row // blk == k, LEAST + table_ref[class_ref[k]], level)
    outer = raw_ref[: 2 * side, : 2 * side] + jnp.where(row == col, level, 0.0)
    out_a[...] = outer - mul_parts(fold, inner_a) - mul_parts(scaled, parts_of(rows_a[...]))
    out_b[...] = -mul_parts(fold, parts_of(rest_b[:side])) - mul_parts(scaled, parts_of(rows_b[...]))


def last_kernel(place_ref, out_a, out_b, scaled_ref, fold_ref, two_c, two_d, three_c, three_d, out_ref):
    side = two_c.shape[0]
    width = 2 * side

    def put(k, value):
        out_ref[:, pl.ds(pl.multiple_of(place_ref[k] * width, width), width)] = value

    put(0, out_a[...])
    put(1, out_b[...])
    scaled = parts_of(scaled_ref[...])
    fold = parts_of(mul_parts(scaled, parts_of(fold_ref[...])))
    for k, two, three, top in ((2, two_c, three_c, 0), (3, two_d, three_d, side)):
        left = [part[:, top : top + side] for part in scaled]
        put(k, mul_parts(fold, parts_of(two[...])) - mul_parts(left, parts_of(three[...])))


def values_kernel(term_ref, half_ref, other_ref, known_ref, inv_ref, inv2_ref, own_ref, sib_ref, out_ref):
    side = inv_ref.shape[0]
    total = jnp.concatenate(
        [term_ref[:side] + half_ref[...], term_ref[side:] + other_ref[...]], axis=0
    )
    face = -mul(inv2_ref[...], total)
    out_ref[:side] = face[:side]
    inner = (
        known_ref[...]
        + mul(own_ref[:side, side:], face[:side])
        + mul(sib_ref[:side, side:], face[side:])
    )
    out_ref[side:] = -mul(inv_ref[...], inner)


def call(kernel, outs, args, specs=None, scratch=(), name=None, flops=0):
    return pl.pallas_call(
        kernel,
        out_shape=[jax.ShapeDtypeStruct(s, f32) for s in outs],
        in_specs=specs or [VM] * len(args),
        out_specs=[VM] * len(outs),
        scratch_shapes=[pltpu.VMEM(s, f32) for s in scratch],
        compiler_params=pltpu.CompilerParams(vmem_limit_bytes=48 * 1024 * 1024),
        cost_estimate=pl.CostEstimate(flops=flops, bytes_accessed=0, transcendentals=0),
        name=name,
    )(*args)


def body(leaf_raw, medium_class, wave_table, boundary_data):
    raw = leaf_raw[0, 0]
    classes = medium_class[0, 0]
    data = boundary_data[0, 0]
    bound = raw.shape[0]
    side = bound // 4
    ncol = data.shape[1]
    half_x = lax.axis_size("gx") // 2
    half_y = lax.axis_size("gy") // 2
    column = lax.axis_index("gx") // half_x
    row = lax.axis_index("gy") // half_y
    place = jnp.stack(
        [2 * row + column, 2 * row + 1 - column, 2 - 2 * row + column, 3 - 2 * row - column]
    ).astype(jnp.int32)

    one, two, three, rest = call(
        pack_kernel,
        [(side + 8, 2 * side), (side, 2 * side), (side, 2 * side), (2 * side + ncol, 2 * side)],
        (classes, wave_table, raw, data),
        [SM, SM, VM, VM],
        name="pack",
    )
    one_x = shifted(one, "gx")
    one_z = shifted(one, "gy")
    rest_x = shifted(rest, "gx")
    two_z = shifted(two, "gy")
    three_z = shifted(three, "gy")
    one_zx = shifted(one_z, "gx")
    two_zx = shifted(two_z, "gx")
    three_zx = shifted(three_z, "gx")

    sq, sq2 = (side, side), (2 * side, 2 * side)
    inv1, fold1, face1 = call(
        own_kernel, [sq, (2 * side, side), sq2], (wave_table, one, one_x), [SM, VM, VM], [sq, sq], "own_level"
    )
    rows_a, rows_b, term, known = call(
        rows_kernel,
        [sq2, sq2, (2 * side, ncol), (side, ncol)],
        (inv1, fold1, rest, rest_x, one, one_x),
        name="pair_rows",
    )
    half_z = shifted(term[:side], "gy")
    half_zx = shifted(half_z, "gx")
    fold2, inv2 = call(
        far_kernel,
        [(2 * side, side), sq2],
        (wave_table, one_z, one_zx, face1),
        [SM, VM, VM, VM],
        [sq, sq, sq, sq2, sq2],
        "far_level",
    )
    out_a, out_b, scaled = call(
        near_kernel,
        [sq2, sq2, sq2],
        (classes, wave_table, raw, rest, rest_x, inv1, inv2, rows_a, rows_b),
        [SM, SM] + [VM] * 7,
        name="near_rows",
    )
    (values,) = call(
        values_kernel,
        [(2 * side, ncol)],
        (term, half_z, half_zx, known, inv1, inv2, one, one_x),
        name="values",
    )
    (parent,) = call(
        last_kernel,
        [(2 * side, 8 * side)],
        (place, out_a, out_b, scaled, fold2, two_z, two_zx, three_z, three_zx),
        [SM] + [VM] * 8,
        name="far_rows",
    )
    return (parent[None, None], values[None, None])


def solution(mesh):
    return jax.shard_map(
        body,
        mesh=mesh,
        in_specs=(P("gx", "gy", None, None), P("gx", "gy", None), P(), P("gx", "gy", None, None)),
        out_specs=(P("gx", "gy", None, None), P("gx", "gy", None, None)),
        check_vma=False,
    )
```

profile of v0, /device:TPU:0, one launch (start us, length us, event | category | flops | bytes accessed | tf_op | source)
XLA Modules:
  0.0 99.9 jit_solution(3489548876754527296)
XLA Ops:
  0.7 1.7 %copy-done = f32[1,1,768,768]{3,2,1,0:T(8,128)S(1)} copy-done((f32[1,1,768,768]{3,2,1,0:T(8,128)S(1)}, f32[1,1,768,768]{3,2,1,0:T(8,128)}, u32[]{:S(2)}) %copy-start) | copy-done | bytes 2359320
  2.3 0.9 copy-done.5
  3.2 0.7 copy-done.8
  3.9 0.7 copy-done.10
  4.6 0.8 pack.1
  5.4 3.0 %collective-permute-start = (f32[512,384]{1,0:T(8,128)S(1)}, f32[512,384]{1,0:T(8,128)S(1)}, u32[]{:S(2)}, u32[]{:S(2)}) collective-permute-start(f32[512,384]{1,0:T(8,128)S(1)} %get-tuple-element.18.rest_a), channel_id=1, source_target_pairs={{0,16},{8,24},{16,0},{24,8},{1,17},{9,25},{17,1},{25,9},{2,18},{10... | collective-permute-start | bytes 2359304 | tf_op jit(solution)/shard_map/ppermute | solution.py:19
  8.4 2.6 %collective-permute-start.2 = (f32[200,384]{1,0:T(8,128)S(1)}, f32[200,384]{1,0:T(8,128)S(1)}, u32[]{:S(2)}, u32[]{:S(2)}) collective-permute-start(f32[200,384]{1,0:T(8,128)S(1)} %get-tuple-element.19.own_ref), channel_id=1, source_target_pairs={{0,4},{1,5},{2,6},{3,7},{4,0},{5,1},{6,2},{7,3},{8,12},{9,13},{10,... | collective-permute-start | bytes 921608 | tf_op jit(solution)/shard_map/ppermute | solution.py:19
  11.3 2.6 %collective-permute-start.6 = (f32[192,384]{1,0:T(8,128)S(1)}, f32[192,384]{1,0:T(8,128)}, u32[]{:S(2)}, u32[]{:S(2)}) collective-permute-start(f32[192,384]{1,0:T(8,128)S(1)} %get-tuple-element.31), channel_id=1, source_target_pairs={{0,4},{1,5},{2,6},{3,7},{4,0},{5,1},{6,2},{7,3},{8,12},{9,13},{10,... | collective-permute-start | bytes 884744 | tf_op jit(solution)/shard_map/ppermute | solution.py:19
  14.4 24.0 %collective-permute-done.2.own_ref = f32[200,384]{1,0:T(8,128)S(1)} collective-permute-done((f32[200,384]{1,0:T(8,128)S(1)}, f32[200,384]{1,0:T(8,128)S(1)}, u32[]{:S(2)}, u32[]{:S(2)}) %collective-permute-start.2) | collective-permute-done | bytes 307232 | tf_op jit(solution)/shard_map/ppermute | solution.py:19
  38.8 6.0 %collective-permute-done.4.two_c = f32[192,384]{1,0:T(8,128)} collective-permute-done((f32[192,384]{1,0:T(8,128)S(1)}, f32[192,384]{1,0:T(8,128)}, u32[]{:S(2)}, u32[]{:S(2)}) %collective-permute-start.4) | collective-permute-done | bytes 294944 | tf_op jit(solution)/shard_map/ppermute | solution.py:19
  45.3 4.7 %collective-permute-done.6.three_c = f32[192,384]{1,0:T(8,128)} collective-permute-done((f32[192,384]{1,0:T(8,128)S(1)}, f32[192,384]{1,0:T(8,128)}, u32[]{:S(2)}, u32[]{:S(2)}) %collective-permute-start.6) | collective-permute-done | bytes 294944 | tf_op jit(solution)/shard_map/ppermute | solution.py:19
  50.5 4.9 %own_level.1 = (f32[192,192]{1,0:T(8,128)S(1)}, f32[384,192]{1,0:T(8,128)S(1)}, f32[384,384]{1,0:T(8,128)S(1)}) custom-call(f32[8]{0:T(128)S(1)} %copy-done.9, f32[200,384]{1,0:T(8,128)S(1)} %get-tuple-element.19.own_ref, f32[200,384]{1,0:T(8,128)S(1)} %collective-permute-done.1.sib_ref), custom_call_target="tpu_custom_call" | custom-call | tf_op jit(solution)/shard_map/own_level/pallas_call | solution.py:272
  55.3 0.8 copy-done.3
  56.1 1.6 %pair_rows.1 = (f32[384,384]{1,0:T(8,128)S(1)}, f32[384,384]{1,0:T(8,128)S(1)}, f32[384,128]{1,0:T(8,128)S(1)}, f32[192,128]{1,0:T(8,128)S(1)}) custom-call(f32[192,192]{1,0:T(8,128)S(1)} %get-tuple-element.20.inv_ref, f32[384,192]{1,0:T(8,128)S(1)} %get-tuple-element.23.fold_ref, f32[512,384]{1,0:T(8,128)S(1)} %get-tuple-element.18.rest_a, ...), custom_call_target="tpu_custom_call" | custom-call | tf_op jit(solution)/shard_map/pair_rows/pallas_call | solution.py:272
  57.7 0.8 copy-done.1
  59.2 0.6 slice.3
  59.9 7.6 %collective-permute-done.8.half_ref = f32[192,128]{1,0:T(8,128)} collective-permute-done((f32[192,128]{1,0:T(8,128)}, f32[192,128]{1,0:T(8,128)}, u32[]{:S(2)}, u32[]{:S(2)}) %collective-permute-start.8) | collective-permute-done | bytes 98336 | tf_op jit(solution)/shard_map/ppermute | solution.py:19
  67.5 1.5 %collective-permute-start.9 = (f32[192,128]{1,0:T(8,128)}, f32[192,128]{1,0:T(8,128)S(1)}, u32[]{:S(2)}, u32[]{:S(2)}) collective-permute-start(f32[192,128]{1,0:T(8,128)} %collective-permute-done.8.half_ref), channel_id=1, source_target_pairs={{0,16},{8,24},{16,0},{24,8},{1,17},{9,25},{17,1},{25,9},{2,18},{10... | collective-permute-start | bytes 294920 | tf_op jit(solution)/shard_map/ppermute | solution.py:19
  69.1 1.1 %copy-done.4 = f32[384,384]{1,0:T(8,128)S(1)} copy-done((f32[384,384]{1,0:T(8,128)S(1)}, f32[384,384]{1,0:T(8,128)}, u32[]{:S(2)}) %copy-start.4) | copy-done | bytes 589848
  70.1 16.3 %far_level.1 = (f32[384,192]{1,0:T(8,128)S(1)}, f32[384,384]{1,0:T(8,128)S(1)}) custom-call(f32[8]{0:T(128)S(1)} %copy-done.9, f32[200,384]{1,0:T(8,128)S(1)} %collective-permute-done.2.own_ref, f32[200,384]{1,0:T(8,128)} %collective-permute-done.3.sib_ref, f32[384,384]{1,0:T(8,128)S(1)} %copy-done.4), custom_call_target="tpu_custom_call" | custom-call | tf_op jit(solution)/shard_map/far_level/pallas_call | solution.py:272
  86.4 1.1 %copy-done.2 = f32[384,384]{1,0:T(8,128)S(1)} copy-done((f32[384,384]{1,0:T(8,128)S(1)}, f32[384,384]{1,0:T(8,128)}, u32[]{:S(2)}) %copy-start.2) | copy-done | bytes 589848
  87.5 4.6 %near_rows.1 = (f32[384,384]{1,0:T(8,128)S(1)}, f32[384,384]{1,0:T(8,128)S(1)}, f32[384,384]{1,0:T(8,128)S(1)}) custom-call(s32[12]{0:T(128)S(1)} %bitcast.13, f32[8]{0:T(128)S(1)} %copy-done.9, f32[768,768]{1,0:T(8,128)} %bitcast.9, f32[512,384]{1,0:T(8,128)S(1)} %get-tuple-element.18.rest_a, f32[512,384]{1,0:T(8,128)S(1)} %collective-permute-done.rest_b, ...), custom_call_target="tpu_custom_call" | custom-call | tf_op jit(solution)/shard_map/near_rows/pallas_call | solution.py:272
  92.1 5.1 %far_rows.1 = f32[384,1536]{1,0:T(8,128)} custom-call(s32[4]{0:T(128)S(1)} %pad_add_fusion.place_ref, f32[384,384]{1,0:T(8,128)S(1)} %get-tuple-element.26.out_a, f32[384,384]{1,0:T(8,128)S(1)} %get-tuple-element.27.out_b, f32[384,384]{1,0:T(8,128)S(1)} %get-tuple-element.28.scaled_ref, f32[384,192]{1,0:T(8,128)S(1)} %get-tuple-element.29.fold_ref, ...), custom_call_target="tpu_custom_call" | custom-call | tf_op jit(solution)/shard_map/far_rows/pallas_call | solution.py:272
  97.2 2.7 %values.1 = f32[384,128]{1,0:T(8,128)} custom-call(f32[384,128]{1,0:T(8,128)S(1)} %get-tuple-element.32.term_ref, f32[192,128]{1,0:T(8,128)} %collective-permute-done.8.half_ref, f32[192,128]{1,0:T(8,128)S(1)} %collective-permute-done.9.other_ref, f32[192,128]{1,0:T(8,128)S(1)} %copy-done.7, f32[192,192]{1,0:T(8,128)S(1)} %get-tuple-element.20.inv_ref, ...), custom_call_target="tpu_custom_call" | custom-call | tf_op jit(solution)/shard_map/values/pallas_call | solution.py:272
  (29 shorter events, 3.0 us)
Async XLA Ops:
  0.6 49.8 %copy-start.9 = (f32[8]{0:T(128)S(1)}, f32[8]{0:T(128)}, u32[]{:S(2)}) copy-start(f32[8]{0:T(128)} %table_ref.7) | copy-start | bytes 100
  0.6 1.7 %copy-start = (f32[1,1,768,768]{3,2,1,0:T(8,128)S(1)}, f32[1,1,768,768]{3,2,1,0:T(8,128)}, u32[]{:S(2)}) copy-start(f32[1,1,768,768]{3,2,1,0:T(8,128)} %param.4) | copy-start | bytes 7077892
  2.3 0.9 copy-start.5
  3.2 0.7 copy-start.8
  3.9 0.7 copy-start.10
  5.4 50.8 %collective-permute-start = (f32[512,384]{1,0:T(8,128)S(1)}, f32[512,384]{1,0:T(8,128)S(1)}, u32[]{:S(2)}, u32[]{:S(2)}) collective-permute-start(f32[512,384]{1,0:T(8,128)S(1)} %get-tuple-element.18.rest_a), channel_id=1, source_target_pairs={{0,16},{8,24},{16,0},{24,8},{1,17},{9,25},{17,1},{25,9},{2,18},{10... | collective-permute-start | bytes 2359304 | tf_op jit(solution)/shard_map/ppermute | solution.py:19
  8.4 30.0 %collective-permute-start.2 = (f32[200,384]{1,0:T(8,128)S(1)}, f32[200,384]{1,0:T(8,128)S(1)}, u32[]{:S(2)}, u32[]{:S(2)}) collective-permute-start(f32[200,384]{1,0:T(8,128)S(1)} %get-tuple-element.19.own_ref), channel_id=1, source_target_pairs={{0,4},{1,5},{2,6},{3,7},{4,0},{5,1},{6,2},{7,3},{8,12},{9,13},{10,... | collective-permute-start | bytes 921608 | tf_op jit(solution)/shard_map/ppermute | solution.py:19
  11.0 33.9 %collective-permute-start.4 = (f32[192,384]{1,0:T(8,128)S(1)}, f32[192,384]{1,0:T(8,128)}, u32[]{:S(2)}, u32[]{:S(2)}) collective-permute-start(f32[192,384]{1,0:T(8,128)S(1)} %get-tuple-element.30), channel_id=1, source_target_pairs={{0,4},{1,5},{2,6},{3,7},{4,0},{5,1},{6,2},{7,3},{8,12},{9,13},{10,... | collective-permute-start | bytes 884744 | tf_op jit(solution)/shard_map/ppermute | solution.py:19
  11.3 75.1 %copy-start.11 = (s32[1,1,12]{2,1,0:T(1,128)S(1)}, s32[1,1,12]{2,1,0:T(1,128)}, u32[]{:S(2)}) copy-start(s32[1,1,12]{2,1,0:T(1,128)} %param.5) | copy-start | bytes 148
  11.3 38.7 %collective-permute-start.6 = (f32[192,384]{1,0:T(8,128)S(1)}, f32[192,384]{1,0:T(8,128)}, u32[]{:S(2)}, u32[]{:S(2)}) collective-permute-start(f32[192,384]{1,0:T(8,128)S(1)} %get-tuple-element.31), channel_id=1, source_target_pairs={{0,4},{1,5},{2,6},{3,7},{4,0},{5,1},{6,2},{7,3},{8,12},{9,13},{10,... | collective-permute-start | bytes 884744 | tf_op jit(solution)/shard_map/ppermute | solution.py:19
  13.9 36.6 %collective-permute-start.1 = (f32[200,384]{1,0:T(8,128)S(1)}, f32[200,384]{1,0:T(8,128)S(1)}, u32[]{:S(2)}, u32[]{:S(2)}) collective-permute-start(f32[200,384]{1,0:T(8,128)S(1)} %get-tuple-element.19.own_ref), channel_id=1, source_target_pairs={{0,16},{8,24},{16,0},{24,8},{1,17},{9,25},{17,1},{25,9},{2,18},{10... | collective-permute-start | bytes 921608 | tf_op jit(solution)/shard_map/ppermute | solution.py:19
  38.4 30.7 %collective-permute-start.3 = (f32[200,384]{1,0:T(8,128)S(1)}, f32[200,384]{1,0:T(8,128)}, u32[]{:S(2)}, u32[]{:S(2)}) collective-permute-start(f32[200,384]{1,0:T(8,128)S(1)} %collective-permute-done.2.own_ref), channel_id=1, source_target_pairs={{0,16},{8,24},{16,0},{24,8},{1,17},{9,25},{17,1},{25,9},{2,18},{10... | collective-permute-start | bytes 921608 | tf_op jit(solution)/shard_map/ppermute | solution.py:19
  44.8 47.3 %collective-permute-start.5 = (f32[192,384]{1,0:T(8,128)}, f32[192,384]{1,0:T(8,128)}, u32[]{:S(2)}, u32[]{:S(2)}) collective-permute-start(f32[192,384]{1,0:T(8,128)} %collective-permute-done.4.two_c), channel_id=1, source_target_pairs={{0,16},{8,24},{16,0},{24,8},{1,17},{9,25},{17,1},{25,9},{2,18},{10... | collective-permute-start | bytes 884744 | tf_op jit(solution)/shard_map/ppermute | solution.py:19
  50.0 42.1 %collective-permute-start.7 = (f32[192,384]{1,0:T(8,128)}, f32[192,384]{1,0:T(8,128)}, u32[]{:S(2)}, u32[]{:S(2)}) collective-permute-start(f32[192,384]{1,0:T(8,128)} %collective-permute-done.6.three_c), channel_id=1, source_target_pairs={{0,16},{8,24},{16,0},{24,8},{1,17},{9,25},{17,1},{25,9},{2,18},{10... | collective-permute-start | bytes 884744 | tf_op jit(solution)/shard_map/ppermute | solution.py:19
  55.3 0.8 copy-start.3
  57.7 0.9 copy-start.1
  58.6 0.6 copy-start.6
  59.9 7.6 %collective-permute-start.8 = (f32[192,128]{1,0:T(8,128)}, f32[192,128]{1,0:T(8,128)}, u32[]{:S(2)}, u32[]{:S(2)}) collective-permute-start(f32[192,128]{1,0:T(8,128)} %slice.3), channel_id=1, source_target_pairs={{0,4},{1,5},{2,6},{3,7},{4,0},{5,1},{6,2},{7,3},{8,12},{9,13},{10,... | collective-permute-start | bytes 294920 | tf_op jit(solution)/shard_map/ppermute | solution.py:19
  67.5 29.7 %collective-permute-start.9 = (f32[192,128]{1,0:T(8,128)}, f32[192,128]{1,0:T(8,128)S(1)}, u32[]{:S(2)}, u32[]{:S(2)}) collective-permute-start(f32[192,128]{1,0:T(8,128)} %collective-permute-done.8.half_ref), channel_id=1, source_target_pairs={{0,16},{8,24},{16,0},{24,8},{1,17},{9,25},{17,1},{25,9},{2,18},{10... | collective-permute-start | bytes 294920 | tf_op jit(solution)/shard_map/ppermute | solution.py:19
  69.1 1.1 %copy-start.4 = (f32[384,384]{1,0:T(8,128)S(1)}, f32[384,384]{1,0:T(8,128)}, u32[]{:S(2)}) copy-start(f32[384,384]{1,0:T(8,128)} %copy-done.3) | copy-start | bytes 1769476
  86.4 1.1 %copy-start.2 = (f32[384,384]{1,0:T(8,128)S(1)}, f32[384,384]{1,0:T(8,128)}, u32[]{:S(2)}) copy-start(f32[384,384]{1,0:T(8,128)} %copy-done.1) | copy-start | bytes 1769476
  92.1 5.1 %copy-start.7 = (f32[192,128]{1,0:T(8,128)S(1)}, f32[192,128]{1,0:T(8,128)}, u32[]{:S(2)}) copy-start(f32[192,128]{1,0:T(8,128)} %copy-done.6) | copy-start | bytes 294916
where the time goes:
time: 100 us; the launch traced here: 99.9 us
  waiting for transfers between devices  42.3 us (42%)
  Pallas kernels  35.9 us (36%)
  starting transfers between devices  11.9 us (12%)
  local copies, waits for them, and re-layouts  8.97 us (9%)
    ppermute x10, waiting for transfers between devices, shifted(): lax.ppermute(shard, axis, [(i, (i + size // 2) % size) for i in range(siz...  42.3 us
    pallas_call x7, Pallas kernels, call(): pl.pallas_call(kernel, out_shape=[jax.ShapeDtypeStruct(s, f32) for s in o...  35.9 us
    ppermute x10, starting transfers between devices, shifted(): lax.ppermute(shard, axis, [(i, (i + size // 2) % size) for i in range(siz...  11.9 us
    unnamed x24, local copies, waits for them, and re-layouts  8.32 us
  transfers between devices with their start and end apart: 10, of which 4 were waited for; matrix products, arithmetic and copies ran while one was open for 1% of the time, Pallas kernels for 32%

commit v1 on v0

v1 whole, which is shorter than its diff:
```python
import functools

import jax
import jax.numpy as jnp
from jax import lax
from jax.experimental import pallas as pl
from jax.experimental.pallas import tpu as pltpu
from jax.sharding import PartitionSpec as P

f32 = jnp.float32
bf16 = jnp.bfloat16
VM = pl.BlockSpec(memory_space=pltpu.VMEM)
ANY = pl.BlockSpec(memory_space=pl.ANY)
HBM = pl.BlockSpec(memory_space=pltpu.HBM)
SM = pl.BlockSpec(memory_space=pltpu.SMEM)
LEAST = 4.0


def shifted(shard, axis):
    size = lax.axis_size(axis)
    return lax.ppermute(shard, axis, [(i, (i + size // 2) % size) for i in range(size)])


def parts_of(x, count=2):
    parts = []
    for _ in range(count - 1):
        parts.append(x.astype(bf16))
        x = x - parts[-1].astype(f32)
    return parts + [x.astype(bf16)]


def dot_of(left, right, contract):
    return lax.dot_general(left, right, (contract, ((), ())), preferred_element_type=f32)


def mul_parts(left, right, contract=((1,), (0,))):
    depth = max(len(left), len(right))
    total = None
    for order in reversed(range(depth)):
        for i in range(order + 1):
            if i < len(left) and order - i < len(right):
                term = dot_of(left[i], right[order - i], contract)
                total = term if total is None else total + term
    return total


def mul(left, right):
    return mul_parts(parts_of(left), parts_of(right))


def mul_t(left, right):
    return mul_parts(parts_of(left), parts_of(right), ((0,), (0,)))


def rows_of(shape):
    return lax.broadcasted_iota(jnp.int32, shape, 0)


def cols_of(shape):
    return lax.broadcasted_iota(jnp.int32, shape, 1)


def eye(n):
    return (rows_of((n, n)) == cols_of((n, n))).astype(f32)


def invert_start(mat, least, inv_ref, res_ref):
    n = mat.shape[0]
    unit = eye(n)
    most = jnp.max(jnp.sum(jnp.abs(mat), axis=0, keepdims=True))
    scale = 2.0 / (most + least)
    eps = (most - least) / (most + least)
    res = unit - scale * mat
    gain = 2.0 / (2.0 - eps * eps)
    inv_ref[...] = (gain * scale) * (unit + res)
    res_parts = parts_of(res)
    res_ref[...] = (1.0 - gain) * unit + gain * mul_parts(res_parts, res_parts)

    def fast(carry):
        eps, noise = carry
        gain = 2.0 / (2.0 - eps * eps)
        inv = inv_ref[...]
        high, low = parts_of(res_ref[...])
        inv_high, inv_low = parts_of(inv)
        if n > 256:
            right_high = jnp.concatenate([high, inv_high], axis=1)
            right_low = jnp.concatenate([low, inv_low], axis=1)
            both = dot_of(
                jnp.concatenate([high, high, low], axis=1),
                jnp.concatenate([right_high, right_low, right_high], axis=0),
                ((1,), (0,)),
            )
            square, step = both[:, :n], both[:, n:]
        else:
            square = mul_parts([high, low], [high, low])
            step = mul_parts([high, low], [inv_high, inv_low])
        inv_ref[...] = gain * (inv + step)
        res_ref[...] = (1.0 - gain) * unit + gain * square
        return gain * eps * eps * 0.5, 2.0 * gain * eps * noise + 3e-5

    eps, noise = lax.while_loop(
        lambda carry: carry[0] > 0.02, fast, (gain * eps * eps * 0.5, jnp.float32(6e-5))
    )
    return jnp.minimum(eps + noise + 1e-5 * (most / least), 0.5)


def invert_end(mat, bound, inv_ref):
    unit = eye(mat.shape[0])
    mat_parts = parts_of(mat, 3)

    def residual(inv_parts):
        return unit - mul_parts(mat_parts, inv_parts)

    def correct(bound):
        inv = inv_ref[...]
        inv_parts = parts_of(inv, 3)
        inv_ref[...] = inv + mul_parts(inv_parts[:2], parts_of(residual(inv_parts)))
        return bound * bound

    lax.while_loop(lambda bound: bound > 0.01, correct, bound)
    inv = inv_ref[...]
    inv_parts = parts_of(inv, 3)
    res_parts = parts_of(residual(inv_parts))
    step = mul_parts(inv_parts[:2], res_parts)
    inv_ref[...] = inv + (step + dot_of(step.astype(bf16), res_parts[0], ((1,), (0,))))


def invert(mat, least, inv_ref, res_ref):
    invert_end(mat, invert_start(mat, least, inv_ref, res_ref), inv_ref)


def pack_kernel(
    class_any, table_any, raw_any, data_any, one_ref, two_ref, three_ref, more_ref,
    classes, table, raw, data, sems,
):
    bound = raw_any.shape[0]
    side = bound // 4
    blk = bound // class_any.shape[0]
    shape = (side, side)
    copies = [
        pltpu.make_async_copy(class_any, classes, sems.at[0]),
        pltpu.make_async_copy(table_any, table, sems.at[1]),
        pltpu.make_async_copy(raw_any.at[pl.ds(2 * side, 2 * side)], raw, sems.at[2]),
        pltpu.make_async_copy(data_any, data, sems.at[3]),
    ]
    for copy in copies:
        copy.start()
    row, col = rows_of(shape), cols_of(shape)
    for copy in copies:
        copy.wait()
    least = table[0]
    for k in range(1, table.shape[0]):
        least = jnp.minimum(least, table[k])

    def level_of(index, start, count):
        level = jnp.zeros(index.shape, f32)
        for k in range(count):
            level = jnp.where(index // blk == k, LEAST + table[classes[start + k]], level)
        return level

    def with_diagonal(block, start):
        return block + jnp.where(row == col, level_of(row, start // blk, side // blk), 0.0)

    face = with_diagonal(raw[:side, 2 * side : 3 * side], 2 * side)
    inner = with_diagonal(raw[side:, 3 * side :], 3 * side)
    one_ref[:side, :side] = jnp.where(row <= col, inner, face)
    one_ref[:side, side:] = raw[side:, 2 * side : 3 * side]
    one_ref[side : side + 8, :] = jnp.zeros((8, 2 * side), f32)
    one_ref[side : side + 1, :side] = jnp.sum(
        jnp.where(row == col, face, 0.0), axis=0, keepdims=True
    )
    one_ref[side + 1 : side + 2, :] = level_of(cols_of((1, 2 * side)), 0, 2 * side // blk)
    one_ref[side + 2 : side + 3, :] = jnp.zeros((1, 2 * side), f32) + 2.0 * (LEAST + least)
    inner_out = raw[side:, : 2 * side]
    two_ref[...] = inner_out
    three_ref[...] = raw[:side, : 2 * side]
    more_ref[:side] = inner_out
    known = mul(inner_out, data[...])
    rows, ncol = more_ref.shape[0] - side, data.shape[1]
    for k in range(side // rows):
        more_ref[side:, k * ncol : (k + 1) * ncol] = known[k * rows : (k + 1) * rows]


def unpack(one_ref):
    side = one_ref.shape[1] // 2
    shape = (side, side)
    row, col = rows_of(shape), cols_of(shape)
    packed = one_ref[:side, :side]
    flipped = packed.T
    inner = jnp.where(row <= col, packed, flipped)
    face = jnp.where(row > col, packed, jnp.where(row < col, flipped, one_ref[side : side + 1, :side]))
    return inner, face, one_ref[:side, side:]


def least_of(one_ref):
    side = one_ref.shape[1] // 2
    return jnp.min(one_ref[side + 2 : side + 3, :])


def pair_level(own_ref, sib_ref, res, inv_ref, fold_ref):
    side = own_ref.shape[1] // 2
    inner_a, face_a, cross_a = unpack(own_ref)
    inner_b, face_b, cross_b = unpack(sib_ref)
    invert(inner_a + inner_b, least_of(own_ref), inv_ref, res)
    inv_parts = parts_of(inv_ref[...])
    parts_a, parts_b = parts_of(cross_a), parts_of(cross_b)
    fold_a = mul_parts(parts_a, inv_parts, ((0,), (0,)))
    fold_b = mul_parts(parts_b, inv_parts, ((0,), (0,)))
    fold_ref[:side] = fold_a
    fold_ref[side:] = fold_b
    fold_a, fold_b = parts_of(fold_a), parts_of(fold_b)
    aa = face_a - mul_parts(fold_a, parts_a)
    ab = -mul_parts(fold_a, parts_b)
    ba = -mul_parts(fold_b, parts_a)
    bb = face_b - mul_parts(fold_b, parts_b)
    return aa, ab, ba, bb


def own_kernel(own_ref, sib_ref, inv_ref, fold_ref, face_ref, res):
    side = own_ref.shape[1] // 2
    aa, ab, ba, bb = pair_level(own_ref, sib_ref, res, inv_ref, fold_ref)
    face_ref[:side, :side] = aa
    face_ref[:side, side:] = ab
    face_ref[side:, :side] = ba
    face_ref[side:, side:] = bb


def far_kernel(own_ref, sib_ref, near_ref, fold_ref, sum_ref, res, inv):
    side = own_ref.shape[1] // 2
    aa, ab, ba, bb = pair_level(own_ref, sib_ref, res, inv, fold_ref)
    sum_ref[:side, :side] = near_ref[:side, :side] + aa
    sum_ref[:side, side:] = near_ref[:side, side:] + ab
    sum_ref[side:, :side] = near_ref[side:, :side] + ba
    sum_ref[side:, side:] = near_ref[side:, side:] + bb


def face_start_kernel(own_ref, sum_ref, inv_ref, bound_ref, res):
    bound = invert_start(sum_ref[...], least_of(own_ref), inv_ref, res)
    bound_ref[...] = jnp.zeros(bound_ref.shape, f32) + bound


def face_end_kernel(sum_ref, start_ref, bound_ref, inv_ref):
    inv_ref[...] = start_ref[...]
    invert_end(sum_ref[...], jnp.max(bound_ref[...]), inv_ref)


def term_kernel(fold_ref, more_a, more_b, three_ref, data_ref, term_ref, known_ref):
    side, ncol = known_ref.shape
    rows = more_a.shape[0] - side
    for k in range(side // rows):
        lanes = slice(k * ncol, (k + 1) * ncol)
        known_ref[k * rows : (k + 1) * rows] = more_a[side:, lanes] + more_b[side:, lanes]
    term_ref[...] = mul(three_ref[...], data_ref[...]) - mul(fold_ref[:side], known_ref[...])


def rows_kernel(
    raw_any, one_ref, fold_ref, inv_ref, more_a, more_b, three_ref, rows_a, rows_b, base_a, base_b,
    outer, sem,
):
    side = inv_ref.shape[0]
    copy = pltpu.make_async_copy(
        raw_any.at[pl.ds(0, 2 * side), pl.ds(0, 2 * side)], outer, sem
    )
    copy.start()
    fold = parts_of(fold_ref[...])
    inner_a, inner_b = parts_of(more_a[:side]), parts_of(more_b[:side])
    rows_a[...] = -mul_parts(fold, inner_a)
    rows_a[:side] += three_ref[...]
    rows_b[...] = -mul_parts(fold, inner_b)
    left = parts_of(mul_parts(inner_a, parts_of(inv_ref[...]), ((0,), (0,))))
    base_b[...] = -mul_parts(left, inner_b)
    shape = (2 * side, 2 * side)
    copy.wait()
    level = jnp.where(rows_of(shape) == cols_of(shape), one_ref[side + 1 : side + 2, :], 0.0)
    base_a[...] = (outer[...] + level) - mul_parts(left, inner_a)


def near_kernel(
    inv2_ref, rows_a, rows_b, base_a, base_b, three_b, fold_ref, out_a, out_b, scaled_ref, mixed_ref
):
    side = three_b.shape[0]
    right = parts_of(rows_a[...])
    scaled = mul_parts(right, parts_of(inv2_ref[...]), ((0,), (0,)))
    scaled_ref[...] = scaled
    scaled = parts_of(scaled)
    mixed_ref[...] = mul_parts(scaled, parts_of(fold_ref[...]))
    out_a[...] = base_a[...] - mul_parts(scaled, right)
    sib = rows_b[...]
    sib = jnp.concatenate([sib[:side], sib[side:] + three_b[...]], axis=0)
    out_b[...] = base_b[...] - mul_parts(scaled, parts_of(sib))


def cross_kernel(scaled_ref, mixed_ref, two_c, two_d, three_c, out_c, out_d):
    side = two_c.shape[0]
    scaled = parts_of(scaled_ref[:, :side])
    mixed = parts_of(mixed_ref[...])
    out_c[...] = mul_parts(mixed, parts_of(two_c[...])) - mul_parts(scaled, parts_of(three_c[...]))
    out_d[...] = mul_parts(mixed, parts_of(two_d[...]))


def last_kernel(place_ref, out_a, out_b, out_c, part_d, scaled_ref, three_d, out_any, out_d, sems):
    side, width = three_d.shape
    copies = []
    for k, ref in enumerate((out_a, out_b, out_c, out_d)):
        lanes = pl.ds(pl.multiple_of(place_ref[k] * width, width), width)
        copies.append(pltpu.make_async_copy(ref, out_any.at[:, lanes], sems.at[k]))
    for copy in copies[:3]:
        copy.start()
    left = parts_of(scaled_ref[:, side:])
    out_d[...] = part_d[...] - mul_parts(left, parts_of(three_d[...]))
    copies[3].start()
    for copy in copies:
        copy.wait()


def values_kernel(total_own, total_sib, known_ref, inv_ref, inv2_ref, own_ref, sib_ref, out_ref):
    side = inv_ref.shape[0]
    face = -mul(inv2_ref[...], jnp.concatenate([total_own[...], total_sib[...]], axis=0))
    out_ref[:side] = face[:side]
    inner = (
        known_ref[...]
        + mul(own_ref[:side, side:], face[:side])
        + mul(sib_ref[:side, side:], face[side:])
    )
    out_ref[side:] = -mul(inv_ref[...], inner)


def call(kernel, outs, args, us, name, specs=None, out_specs=None, scratch=()):
    return pl.pallas_call(
        kernel,
        out_shape=[jax.ShapeDtypeStruct(s, f32) for s in outs],
        in_specs=specs or [VM] * len(args),
        out_specs=out_specs or [VM] * len(outs),
        scratch_shapes=[pltpu.VMEM(s, f32) if isinstance(s, tuple) else s for s in scratch],
        compiler_params=pltpu.CompilerParams(vmem_limit_bytes=12 * 1024 * 1024),
        cost_estimate=pl.CostEstimate(flops=int(us * 3e8), bytes_accessed=0, transcendentals=0),
        name=name,
    )(*args)


def in_hbm(array):
    return pltpu.with_memory_space_constraint(array, pltpu.HBM)


def after(arrays, done):
    return lax.optimization_barrier((*arrays, done))


def body(leaf_raw, medium_class, wave_table, boundary_data):
    raw = leaf_raw[0, 0]
    classes = medium_class[0, 0]
    data = boundary_data[0, 0]
    bound = raw.shape[0]
    side = bound // 4
    ncol = data.shape[1]
    half_x = lax.axis_size("gx") // 2
    half_y = lax.axis_size("gy") // 2
    column = lax.axis_index("gx") // half_x
    row = lax.axis_index("gy") // half_y
    place = jnp.stack(
        [2 * row + column, 2 * row + 1 - column, 2 - 2 * row + column, 3 - 2 * row - column]
    ).astype(jnp.int32)
    sq, sq2, wide, thin = (side, side), (2 * side, 2 * side), (side, 2 * side), (2 * side, side)
    narrow = (side, ncol)

    one, two, three, more = call(
        pack_kernel,
        [(side + 8, 2 * side), wide, wide, (side + ncol // 2, 2 * side)],
        tuple(in_hbm(x) for x in (classes, wave_table, raw, data)),
        2,
        "pack",
        specs=[HBM] * 4,
        scratch=[
            pltpu.SMEM(classes.shape, jnp.int32),
            pltpu.SMEM(wave_table.shape, f32),
            (2 * side, bound),
            data.shape,
            pltpu.SemaphoreType.DMA((4,)),
        ],
    )
    one_z = shifted(one, "gy")
    one_x = shifted(one, "gx")
    more_s, one_x = after((more,), one_x)
    more_x = shifted(more_s, "gx")
    inv1, fold1, face1 = call(
        own_kernel, [sq, thin, sq2], (one, one_x), 5, "own_level", scratch=[sq]
    )
    two_s, one_z, inv1 = after((two, one_z), inv1)
    two_z = shifted(two_s, "gy")
    one_zx = shifted(one_z, "gx")
    term, known = call(
        term_kernel, [narrow] * 2, (fold1, more, more_x, three, data), 1, "own_term"
    )
    three_s, more_x, term = after((three, more_x), term)
    three_z = shifted(three_s, "gy")
    rows_a, rows_b, base_a, base_b = call(
        rows_kernel,
        [sq2] * 4,
        (in_hbm(raw), one, fold1, inv1, more, more_x, three),
        2,
        "pair_rows",
        specs=[HBM] + [VM] * 6,
        scratch=[sq2, pltpu.SemaphoreType.DMA(())],
    )
    one_zx, rows_a = after((one_zx,), rows_a)
    three_s, one_zx = after((three,), one_zx)
    three_x = shifted(three_s, "gx")
    fold2, sum2 = call(
        far_kernel, [thin, sq2], (one_z, one_zx, face1), 6, "far_level", scratch=[sq, sq]
    )
    start2, bound2 = call(
        face_start_kernel, [sq2, (8, 128)], (one, sum2), 6, "face_start", scratch=[sq2]
    )
    term_s, start2 = after((term,), start2)
    term_z = shifted(term_s, "gy")
    two_z, start2 = after((two_z,), start2)
    two_zx = shifted(two_z, "gx")
    start2, two_z = after((start2,), two_z)
    (inv2,) = call(face_end_kernel, [sq2], (sum2, start2, bound2), 4, "face_end")
    three_z, inv2 = after((three_z,), inv2)
    three_zx = shifted(three_z, "gx")
    out_a, out_b, scaled, mixed = call(
        near_kernel,
        [sq2, sq2, sq2, thin],
        (inv2, rows_a, rows_b, base_a, base_b, three_x, fold2),
        3,
        "near_rows",
    )
    term_z, scaled = after((term_z,), scaled)
    total = term + term_z
    total_x = shifted(total, "gx")
    out_c, part_d = call(
        cross_kernel, [sq2, sq2], (scaled, mixed, two_z, two_zx, three_z), 2, "cross_rows"
    )
    (values,) = call(
        values_kernel,
        [(2 * side, ncol)],
        (total, total_x, known, inv1, inv2, one, one_x),
        2,
        "values",
    )
    (parent,) = call(
        last_kernel,
        [(2 * side, 8 * side)],
        (place, out_a, out_b, out_c, part_d, scaled, three_zx),
        2,
        "last_rows",
        specs=[SM] + [VM] * 6,
        out_specs=[ANY],
        scratch=[sq2, pltpu.SemaphoreType.DMA((4,))],
    )
    return (parent[None, None], values[None, None])


def solution(mesh):
    return jax.shard_map(
        body,
        mesh=mesh,
        in_specs=(P("gx", "gy", None, None), P("gx", "gy", None), P(), P("gx", "gy", None, None)),
        out_specs=(P("gx", "gy", None, None), P("gx", "gy", None, None)),
        check_vma=False,
    )
```

time: 100 us -> 65.3 us (0.65)
  waiting for transfers between devices: 42.3 us -> 21.6 us
  Pallas kernels: 35.9 us -> 26.5 us
  local copies, waits for them, and re-layouts: 8.97 us -> 0.82 us
  starting transfers between devices: 11.9 us -> 15.2 us
    ppermute x10 -> x11, waiting for transfers between devices: 42.3 us -> 21.6 us  [shifted(): lax.ppermute(shard, axis, [(i, (i + size // 2) % size) for i in range(siz...]
    pallas_call x7 -> x11, Pallas kernels: 35.9 us -> 26.5 us  [call(): pl.pallas_call(kernel, out_shape=[jax.ShapeDtypeStruct(s, f32) for s in o...]
    unnamed x24 -> x6, local copies, waits for them, and re-layouts: 8.32 us -> 0.82 us
    ppermute x10 -> x11, starting transfers between devices: 11.9 us -> 15.2 us  [shifted(): lax.ppermute(shard, axis, [(i, (i + size // 2) % size) for i in range(siz...]
  transfers between devices with their start and end apart: 10 -> 11, of which waited for: 4 -> 7; matrix products, arithmetic and copies ran while one was open for 1% -> 0% of each run, Pallas kernels for 32% -> 35%
where the time goes in v1:
time: 65.3 us; the launch traced here: 65.1 us
  Pallas kernels  26.5 us (41%)
  waiting for transfers between devices  21.6 us (33%)
  starting transfers between devices  15.2 us (23%)
  between operations  0.9 us (1%)
  local copies, waits for them, and re-layouts  0.82 us (1%)
    pallas_call x11, Pallas kernels, call(): pl.pallas_call(kernel, out_shape=[jax.ShapeDtypeStruct(s, f32) for s in o...  26.5 us
    ppermute x11, waiting for transfers between devices, shifted(): lax.ppermute(shard, axis, [(i, (i + size // 2) % size) for i in range(siz...  21.6 us
    ppermute x11, starting transfers between devices, shifted(): lax.ppermute(shard, axis, [(i, (i + size // 2) % size) for i in range(siz...  15.2 us
  transfers between devices with their start and end apart: 11, of which 7 were waited for; matrix products, arithmetic and copies ran while one was open for 0% of the time, Pallas kernels for 35%

profile of v1, /device:TPU:0, one launch (start us, length us, event | category | flops | bytes accessed | tf_op | source)
XLA Modules:
  0.0 65.1 jit_solution(4144874581845600420)
XLA Ops:
  0.6 1.7 %pack.1 = (f32[200,384]{1,0:T(8,128)S(1)}, f32[192,384]{1,0:T(8,128)S(1)}, f32[192,384]{1,0:T(8,128)S(1)}, f32[256,384]{1,0:T(8,128)S(1)}) custom-call(s32[12]{0:T(128)} %bitcast.14, f32[8]{0:T(128)} %table_any.1, f32[768,768]{1,0:T(8,128)} %bitcast.11, f32[384,128]{1,0:T(8,128)} %bitcast.9), custom_call_target="tpu_custom_call" | custom-call | flops 600000000 | tf_op jit(solution)/shard_map/pack/pallas_call | solution.py:329
  2.3 3.0 %collective-permute-start = (f32[200,384]{1,0:T(8,128)S(1)}, f32[200,384]{1,0:T(8,128)S(1)}, u32[]{:S(2)}, u32[]{:S(2)}) collective-permute-start(f32[200,384]{1,0:T(8,128)S(1)} %get-tuple-element.49.own_ref.one_ref), channel_id=1, source_target_pairs={{0,16},{8,24},{16,0},{24,8},{1,17},{9,25},{17,1},{25,9},{2,18},{10... | collective-permute-start | bytes 921608 | tf_op jit(solution)/shard_map/ppermute | solution.py:21
  5.3 2.6 %collective-permute-start.3 = (f32[200,384]{1,0:T(8,128)S(1)}, f32[200,384]{1,0:T(8,128)S(1)}, u32[]{:S(2)}, u32[]{:S(2)}) collective-permute-start(f32[200,384]{1,0:T(8,128)S(1)} %get-tuple-element.49.own_ref.one_ref), channel_id=1, source_target_pairs={{0,4},{1,5},{2,6},{3,7},{4,0},{5,1},{6,2},{7,3},{8,12},{9,13},{10,... | collective-permute-start | bytes 921608 | tf_op jit(solution)/shard_map/ppermute | solution.py:21
  7.9 4.7 %collective-permute-done.sib_ref = f32[200,384]{1,0:T(8,128)S(1)} collective-permute-done((f32[200,384]{1,0:T(8,128)S(1)}, f32[200,384]{1,0:T(8,128)S(1)}, u32[]{:S(2)}, u32[]{:S(2)}) %collective-permute-start) | collective-permute-done | bytes 307232 | tf_op jit(solution)/shard_map/ppermute | solution.py:21
  12.6 1.7 %collective-permute-start.1 = (f32[256,384]{1,0:T(8,128)S(1)}, f32[256,384]{1,0:T(8,128)S(1)}, u32[]{:S(2)}, u32[]{:S(2)}) collective-permute-start(f32[256,384]{1,0:T(8,128)S(1)} %get-tuple-element.50.more_a), channel_id=1, source_target_pairs={{0,16},{8,24},{16,0},{24,8},{1,17},{9,25},{17,1},{25,9},{2,18},{10... | collective-permute-start | bytes 1179656 | tf_op jit(solution)/shard_map/ppermute | solution.py:21
  14.3 3.6 %own_level.1 = (f32[192,192]{1,0:T(8,128)S(1)}, f32[384,192]{1,0:T(8,128)S(1)}, f32[384,384]{1,0:T(8,128)S(1)}) custom-call(f32[200,384]{1,0:T(8,128)S(1)} %get-tuple-element.49.own_ref.one_ref, f32[200,384]{1,0:T(8,128)S(1)} %collective-permute-done.sib_ref), custom_call_target="tpu_custom_call" | custom-call | flops 1500000000 | tf_op jit(solution)/shard_map/own_level/pallas_call | solution.py:329
  18.7 2.8 %collective-permute-done.3.own_ref = f32[200,384]{1,0:T(8,128)S(1)} collective-permute-done((f32[200,384]{1,0:T(8,128)S(1)}, f32[200,384]{1,0:T(8,128)S(1)}, u32[]{:S(2)}, u32[]{:S(2)}) %collective-permute-start.3) | collective-permute-done | bytes 307232 | tf_op jit(solution)/shard_map/ppermute | solution.py:21
  22.0 0.9 %collective-permute-done.1.more_b = f32[256,384]{1,0:T(8,128)S(1)} collective-permute-done((f32[256,384]{1,0:T(8,128)S(1)}, f32[256,384]{1,0:T(8,128)S(1)}, u32[]{:S(2)}, u32[]{:S(2)}) %collective-permute-start.1) | collective-permute-done | bytes 393248 | tf_op jit(solution)/shard_map/ppermute | solution.py:21
  23.3 2.4 %pair_rows.1 = (f32[384,384]{1,0:T(8,128)S(1)}, f32[384,384]{1,0:T(8,128)S(1)}, f32[384,384]{1,0:T(8,128)S(1)}, f32[384,384]{1,0:T(8,128)S(1)}) custom-call(f32[768,768]{1,0:T(8,128)} %bitcast.12, f32[200,384]{1,0:T(8,128)S(1)} %get-tuple-element.49.own_ref.one_ref, f32[384,192]{1,0:T(8,128)S(1)} %get-tuple-element.52.fold_ref, ...), custom_call_target="tpu_custom_call" | custom-call | flops 600000000 | tf_op jit(solution)/shard_map/pair_rows/pallas_call | solution.py:329
  25.7 4.0 %collective-permute-done.4.sib_ref = f32[200,384]{1,0:T(8,128)S(1)} collective-permute-done((f32[200,384]{1,0:T(8,128)S(1)}, f32[200,384]{1,0:T(8,128)S(1)}, u32[]{:S(2)}, u32[]{:S(2)}) %collective-permute-start.4) | collective-permute-done | bytes 307232 | tf_op jit(solution)/shard_map/ppermute | solution.py:21
  29.6 2.3 %collective-permute-start.2 = (f32[192,384]{1,0:T(8,128)S(1)}, f32[192,384]{1,0:T(8,128)S(1)}, u32[]{:S(2)}, u32[]{:S(2)}) collective-permute-start(f32[192,384]{1,0:T(8,128)S(1)} %get-tuple-element.78.three_ref), channel_id=1, source_target_pairs={{0,4},{1,5},{2,6},{3,7},{4,0},{5,1},{6,2},{7,3},{8,12},{9,13},{10,... | collective-permute-start | bytes 884744 | tf_op jit(solution)/shard_map/ppermute | solution.py:21
  32.0 1.5 %collective-permute-start.6 = (f32[192,384]{1,0:T(8,128)S(1)}, f32[192,384]{1,0:T(8,128)S(1)}, u32[]{:S(2)}, u32[]{:S(2)}) collective-permute-start(f32[192,384]{1,0:T(8,128)S(1)} %get-tuple-element.78.three_ref), channel_id=1, source_target_pairs={{0,16},{8,24},{16,0},{24,8},{1,17},{9,25},{17,1},{25,9},{2,18},{10... | collective-permute-start | bytes 884744 | tf_op jit(solution)/shard_map/ppermute | solution.py:21
  33.5 3.5 %far_level.1 = (f32[384,192]{1,0:T(8,128)S(1)}, f32[384,384]{1,0:T(8,128)S(1)}) custom-call(f32[200,384]{1,0:T(8,128)S(1)} %collective-permute-done.3.own_ref, f32[200,384]{1,0:T(8,128)S(1)} %collective-permute-done.4.sib_ref, f32[384,384]{1,0:T(8,128)S(1)} %copy-done.2), custom_call_target="tpu_custom_call" | custom-call | flops 1800000000 | tf_op jit(solution)/shard_map/far_level/pallas_call | solution.py:329
  37.0 4.9 %face_start.1 = (f32[384,384]{1,0:T(8,128)S(1)}, f32[8,128]{1,0:T(8,128)S(1)}) custom-call(f32[200,384]{1,0:T(8,128)S(1)} %get-tuple-element.49.own_ref.one_ref, f32[384,384]{1,0:T(8,128)S(1)} %get-tuple-element.64.sum_ref), custom_call_target="tpu_custom_call" | custom-call | flops 1800000000 | tf_op jit(solution)/shard_map/face_start/pallas_call | solution.py:329
  41.9 3.3 %collective-permute-done.5.two_c = f32[192,384]{1,0:T(8,128)S(1)} collective-permute-done((f32[192,384]{1,0:T(8,128)S(1)}, f32[192,384]{1,0:T(8,128)S(1)}, u32[]{:S(2)}, u32[]{:S(2)}) %collective-permute-start.5) | collective-permute-done | bytes 294944 | tf_op jit(solution)/shard_map/ppermute | solution.py:21
  45.2 1.5 %collective-permute-start.8 = (f32[192,384]{1,0:T(8,128)S(1)}, f32[192,384]{1,0:T(8,128)S(1)}, u32[]{:S(2)}, u32[]{:S(2)}) collective-permute-start(f32[192,384]{1,0:T(8,128)S(1)} %collective-permute-done.5.two_c), channel_id=1, source_target_pairs={{0,16},{8,24},{16,0},{24,8},{1,17},{9,25},{17,1},{25,9},{2,18},{10... | collective-permute-start | bytes 884744 | tf_op jit(solution)/shard_map/ppermute | solution.py:21
  46.7 2.9 %face_end.1.inv2_ref = f32[384,384]{1,0:T(8,128)S(1)} custom-call(f32[384,384]{1,0:T(8,128)S(1)} %get-tuple-element.64.sum_ref, f32[384,384]{1,0:T(8,128)S(1)} %get-tuple-element.71.start_ref, f32[8,128]{1,0:T(8,128)S(1)} %get-tuple-element.72.bound_ref), custom_call_target="tpu_custom_call" | custom-call | flops 1200000000 | tf_op jit(solution)/shard_map/face_end/pallas_call | solution.py:329
  49.6 3.0 %collective-permute-done.2.three_c = f32[192,384]{1,0:T(8,128)S(1)} collective-permute-done((f32[192,384]{1,0:T(8,128)S(1)}, f32[192,384]{1,0:T(8,128)S(1)}, u32[]{:S(2)}, u32[]{:S(2)}) %collective-permute-start.2) | collective-permute-done | bytes 294944 | tf_op jit(solution)/shard_map/ppermute | solution.py:21
  52.6 1.5 %collective-permute-start.9 = (f32[192,384]{1,0:T(8,128)S(1)}, f32[192,384]{1,0:T(8,128)S(1)}, u32[]{:S(2)}, u32[]{:S(2)}) collective-permute-start(f32[192,384]{1,0:T(8,128)S(1)} %collective-permute-done.2.three_c), channel_id=1, source_target_pairs={{0,16},{8,24},{16,0},{24,8},{1,17},{9,25},{17,1},{25,9},{2,18},{10... | collective-permute-start | bytes 884744 | tf_op jit(solution)/shard_map/ppermute | solution.py:21
  54.1 2.3 %near_rows.1 = (f32[384,384]{1,0:T(8,128)S(1)}, f32[384,384]{1,0:T(8,128)S(1)}, f32[384,384]{1,0:T(8,128)S(1)}, f32[384,192]{1,0:T(8,128)S(1)}) custom-call(f32[384,384]{1,0:T(8,128)S(1)} %face_end.1.inv2_ref, f32[384,384]{1,0:T(8,128)S(1)} %get-tuple-element.74.rows_a, f32[384,384]{1,0:T(8,128)S(1)} %get-tuple-element.75.rows_b, ...), custom_call_target="tpu_custom_call" | custom-call | flops 900000000 | tf_op jit(solution)/shard_map/near_rows/pallas_call | solution.py:329
  57.2 1.1 %cross_rows.1 = (f32[384,384]{1,0:T(8,128)S(1)}, f32[384,384]{1,0:T(8,128)S(1)}) custom-call(f32[384,384]{1,0:T(8,128)S(1)} %get-tuple-element.84.scaled_ref, f32[384,192]{1,0:T(8,128)S(1)} %get-tuple-element.85.mixed_ref, f32[192,384]{1,0:T(8,128)S(1)} %collective-permute-done.5.two_c, f32[192,384]{1,0:T(8,128)S(1)} %collective-permute-done.8.two_d, ...), custom_call_target="tpu_custom_call" | custom-call | flops 600000000 | tf_op jit(solution)/shard_map/cross_rows/pallas_call | solution.py:329
  58.3 2.9 %collective-permute-done.10.total_sib = f32[192,128]{1,0:T(8,128)S(1)} collective-permute-done((f32[192,128]{1,0:T(8,128)S(1)}, f32[192,128]{1,0:T(8,128)S(1)}, u32[]{:S(2)}, u32[]{:S(2)}) %collective-permute-start.10) | collective-permute-done | bytes 98336 | tf_op jit(solution)/shard_map/ppermute | solution.py:21
  61.2 1.8 %values.1 = f32[384,128]{1,0:T(8,128)} custom-call(f32[192,128]{1,0:T(8,128)S(1)} %add.17.total_own, f32[192,128]{1,0:T(8,128)S(1)} %collective-permute-done.10.total_sib, f32[192,128]{1,0:T(8,128)S(1)} %get-tuple-element.91.known_ref, f32[192,192]{1,0:T(8,128)S(1)} %get-tuple-element.58.inv_ref, f32[384,384]{1,0:T(8,128)S(1)} %face_end.1.inv2_ref, ...), custom_call_target="tpu_custom_call" | custom-call | flops 600000000 | tf_op jit(solution)/shard_map/values/pallas_call | solution.py:329
  63.0 2.0 %last_rows.1 = f32[384,1536]{1,0:T(8,128)} custom-call(s32[4]{0:T(128)S(1)} %pad_add_fusion.place_ref, f32[384,384]{1,0:T(8,128)S(1)} %get-tuple-element.80.out_a, f32[384,384]{1,0:T(8,128)S(1)} %get-tuple-element.81.out_b, f32[384,384]{1,0:T(8,128)S(1)} %get-tuple-element.88.out_c, f32[384,384]{1,0:T(8,128)S(1)} %get-tuple-element.89.part_d, ...), custom_call_target="tpu_custom_call" | custom-call | flops 600000000 | tf_op jit(solution)/shard_map/last_rows/pallas_call | solution.py:329
  (17 shorter events, 2.3 us)
Async XLA Ops:
  2.3 10.3 %collective-permute-start = (f32[200,384]{1,0:T(8,128)S(1)}, f32[200,384]{1,0:T(8,128)S(1)}, u32[]{:S(2)}, u32[]{:S(2)}) collective-permute-start(f32[200,384]{1,0:T(8,128)S(1)} %get-tuple-element.49.own_ref.one_ref), channel_id=1, source_target_pairs={{0,16},{8,24},{16,0},{24,8},{1,17},{9,25},{17,1},{25,9},{2,18},{10... | collective-permute-start | bytes 921608 | tf_op jit(solution)/shard_map/ppermute | solution.py:21
  5.3 16.2 %collective-permute-start.3 = (f32[200,384]{1,0:T(8,128)S(1)}, f32[200,384]{1,0:T(8,128)S(1)}, u32[]{:S(2)}, u32[]{:S(2)}) collective-permute-start(f32[200,384]{1,0:T(8,128)S(1)} %get-tuple-element.49.own_ref.one_ref), channel_id=1, source_target_pairs={{0,4},{1,5},{2,6},{3,7},{4,0},{5,1},{6,2},{7,3},{8,12},{9,13},{10,... | collective-permute-start | bytes 921608 | tf_op jit(solution)/shard_map/ppermute | solution.py:21
  12.6 10.3 %copy-start = (f32[1,1,384,128]{3,2,1,0:T(8,128)S(1)}, f32[1,1,384,128]{3,2,1,0:T(8,128)}, u32[]{:S(2)}) copy-start(f32[1,1,384,128]{3,2,1,0:T(8,128)} %param.7) | copy-start | bytes 589828
  12.6 10.3 %collective-permute-start.1 = (f32[256,384]{1,0:T(8,128)S(1)}, f32[256,384]{1,0:T(8,128)S(1)}, u32[]{:S(2)}, u32[]{:S(2)}) collective-permute-start(f32[256,384]{1,0:T(8,128)S(1)} %get-tuple-element.50.more_a), channel_id=1, source_target_pairs={{0,16},{8,24},{16,0},{24,8},{1,17},{9,25},{17,1},{25,9},{2,18},{10... | collective-permute-start | bytes 1179656 | tf_op jit(solution)/shard_map/ppermute | solution.py:21
  17.9 0.8 %copy-start.1 = (f32[384,384]{1,0:T(8,128)}, f32[384,384]{1,0:T(8,128)S(1)}, u32[]{:S(2)}) copy-start(f32[384,384]{1,0:T(8,128)S(1)} %get-tuple-element.63.near_ref) | copy-start | bytes 1769476
  21.5 8.1 %collective-permute-start.4 = (f32[200,384]{1,0:T(8,128)S(1)}, f32[200,384]{1,0:T(8,128)S(1)}, u32[]{:S(2)}, u32[]{:S(2)}) collective-permute-start(f32[200,384]{1,0:T(8,128)S(1)} %collective-permute-done.3.own_ref), channel_id=1, source_target_pairs={{0,16},{8,24},{16,0},{24,8},{1,17},{9,25},{17,1},{25,9},{2,18},{10... | collective-permute-start | bytes 921608 | tf_op jit(solution)/shard_map/ppermute | solution.py:21
  22.0 23.2 %collective-permute-start.5 = (f32[192,384]{1,0:T(8,128)S(1)}, f32[192,384]{1,0:T(8,128)S(1)}, u32[]{:S(2)}, u32[]{:S(2)}) collective-permute-start(f32[192,384]{1,0:T(8,128)S(1)} %get-tuple-element.65), channel_id=1, source_target_pairs={{0,4},{1,5},{2,6},{3,7},{4,0},{5,1},{6,2},{7,3},{8,12},{9,13},{10,... | collective-permute-start | bytes 884744 | tf_op jit(solution)/shard_map/ppermute | solution.py:21
  23.2 10.2 %copy-start.2 = (f32[384,384]{1,0:T(8,128)S(1)}, f32[384,384]{1,0:T(8,128)}, u32[]{:S(2)}) copy-start(f32[384,384]{1,0:T(8,128)} %copy-done.1) | copy-start | bytes 1769476
  29.6 23.0 %collective-permute-start.2 = (f32[192,384]{1,0:T(8,128)S(1)}, f32[192,384]{1,0:T(8,128)S(1)}, u32[]{:S(2)}, u32[]{:S(2)}) collective-permute-start(f32[192,384]{1,0:T(8,128)S(1)} %get-tuple-element.78.three_ref), channel_id=1, source_target_pairs={{0,4},{1,5},{2,6},{3,7},{4,0},{5,1},{6,2},{7,3},{8,12},{9,13},{10,... | collective-permute-start | bytes 884744 | tf_op jit(solution)/shard_map/ppermute | solution.py:21
  32.0 22.2 %collective-permute-start.6 = (f32[192,384]{1,0:T(8,128)S(1)}, f32[192,384]{1,0:T(8,128)S(1)}, u32[]{:S(2)}, u32[]{:S(2)}) collective-permute-start(f32[192,384]{1,0:T(8,128)S(1)} %get-tuple-element.78.three_ref), channel_id=1, source_target_pairs={{0,16},{8,24},{16,0},{24,8},{1,17},{9,25},{17,1},{25,9},{2,18},{10... | collective-permute-start | bytes 884744 | tf_op jit(solution)/shard_map/ppermute | solution.py:21
  45.2 11.9 %collective-permute-start.8 = (f32[192,384]{1,0:T(8,128)S(1)}, f32[192,384]{1,0:T(8,128)S(1)}, u32[]{:S(2)}, u32[]{:S(2)}) collective-permute-start(f32[192,384]{1,0:T(8,128)S(1)} %collective-permute-done.5.two_c), channel_id=1, source_target_pairs={{0,16},{8,24},{16,0},{24,8},{1,17},{9,25},{17,1},{25,9},{2,18},{10... | collective-permute-start | bytes 884744 | tf_op jit(solution)/shard_map/ppermute | solution.py:21
  46.7 9.7 %collective-permute-start.7 = (f32[192,128]{1,0:T(8,128)S(1)}, f32[192,128]{1,0:T(8,128)S(1)}, u32[]{:S(2)}, u32[]{:S(2)}) collective-permute-start(f32[192,128]{1,0:T(8,128)S(1)} %get-tuple-element.82), channel_id=1, source_target_pairs={{0,4},{1,5},{2,6},{3,7},{4,0},{5,1},{6,2},{7,3},{8,12},{9,13},{10,... | collective-permute-start | bytes 294920 | tf_op jit(solution)/shard_map/ppermute | solution.py:21
  52.6 10.4 %collective-permute-start.9 = (f32[192,384]{1,0:T(8,128)S(1)}, f32[192,384]{1,0:T(8,128)S(1)}, u32[]{:S(2)}, u32[]{:S(2)}) collective-permute-start(f32[192,384]{1,0:T(8,128)S(1)} %collective-permute-done.2.three_c), channel_id=1, source_target_pairs={{0,16},{8,24},{16,0},{24,8},{1,17},{9,25},{17,1},{25,9},{2,18},{10... | collective-permute-start | bytes 884744 | tf_op jit(solution)/shard_map/ppermute | solution.py:21
  56.5 4.7 %collective-permute-start.10 = (f32[192,128]{1,0:T(8,128)S(1)}, f32[192,128]{1,0:T(8,128)S(1)}, u32[]{:S(2)}, u32[]{:S(2)}) collective-permute-start(f32[192,128]{1,0:T(8,128)S(1)} %add.17.total_own), channel_id=1, source_target_pairs={{0,16},{8,24},{16,0},{24,8},{1,17},{9,25},{17,1},{25,9},{2,18},{10... | collective-permute-start | bytes 294920 | tf_op jit(solution)/shard_map/ppermute | solution.py:21

commit v2 on v1

--- a/solution.py
+++ b/solution.py
@@ -130,7 +130,7 @@
 
 
 def pack_kernel(
-    class_any, table_any, raw_any, data_any, one_ref, two_ref, three_ref, more_ref,
+    class_any, table_any, raw_any, data_any, one_ref, two_ref, three_ref, four_ref, face_ref, more_ref,
     classes, table, raw, data, sems,
 ):
     bound = raw_any.shape[0]
@@ -172,8 +172,12 @@
     one_ref[side + 1 : side + 2, :] = level_of(cols_of((1, 2 * side)), 0, 2 * side // blk)
     one_ref[side + 2 : side + 3, :] = jnp.zeros((1, 2 * side), f32) + 2.0 * (LEAST + least)
     inner_out = raw[side:, : 2 * side]
-    two_ref[...] = inner_out
-    three_ref[...] = raw[:side, : 2 * side]
+    face_ref[...] = raw[:side, : 2 * side]
+    outer = jnp.concatenate([inner_out, raw[:side, : 2 * side]], axis=0)
+    cut = 0
+    for ref in (two_ref, three_ref, four_ref):
+        ref[...] = outer[cut : cut + ref.shape[0]]
+        cut = cut + ref.shape[0]
     more_ref[:side] = inner_out
     known = mul(inner_out, data[...])
     rows, ncol = more_ref.shape[0] - side, data.shape[1]
@@ -254,86 +258,142 @@
 
 
 def rows_kernel(
-    raw_any, one_ref, fold_ref, inv_ref, more_a, more_b, three_ref, rows_a, rows_b, base_a, base_b,
-    outer, sem,
+    raw_any, one_ref, fold_ref, inv_ref, more_a, more_b, three_ref, known_ref,
+    rows_a, rows_b, base_a, base_b, fold_any, shift_any, outer, shift, sems,
 ):
     side = inv_ref.shape[0]
     copy = pltpu.make_async_copy(
-        raw_any.at[pl.ds(0, 2 * side), pl.ds(0, 2 * side)], outer, sem
+        raw_any.at[pl.ds(0, 2 * side), pl.ds(0, 2 * side)], outer, sems.at[0]
     )
     copy.start()
+    fold_store = pltpu.make_async_copy(fold_ref, fold_any, sems.at[1])
+    fold_store.start()
     fold = parts_of(fold_ref[...])
+    inverse = parts_of(inv_ref[...])
+    shift[...] = -mul_parts(inverse, parts_of(known_ref[...]))
+    shift_store = pltpu.make_async_copy(shift, shift_any, sems.at[2])
+    shift_store.start()
     inner_a, inner_b = parts_of(more_a[:side]), parts_of(more_b[:side])
     rows_a[...] = -mul_parts(fold, inner_a)
     rows_a[:side] += three_ref[...]
     rows_b[...] = -mul_parts(fold, inner_b)
-    left = parts_of(mul_parts(inner_a, parts_of(inv_ref[...]), ((0,), (0,))))
+    left = parts_of(mul_parts(inner_a, inverse, ((0,), (0,))))
     base_b[...] = -mul_parts(left, inner_b)
     shape = (2 * side, 2 * side)
     copy.wait()
     level = jnp.where(rows_of(shape) == cols_of(shape), one_ref[side + 1 : side + 2, :], 0.0)
     base_a[...] = (outer[...] + level) - mul_parts(left, inner_a)
+    fold_store.wait()
+    shift_store.wait()
+
+
+def pieces(source, target, sems, start, lanes=slice(None), count=4):
+    rows = source.shape[0] // count
+    return [
+        pltpu.make_async_copy(
+            source.at[pl.ds(k * rows, rows)], target.at[pl.ds(k * rows, rows), lanes], sems.at[start + k]
+        )
+        for k in range(count)
+    ]
+
+
+def lanes_of(place_ref, k, width):
+    return pl.ds(pl.multiple_of(place_ref[k] * width, width), width)
+
+
+def start_all(copies):
+    for copy in copies:
+        copy.start()
+
+
+def wait_all(copies):
+    for copy in copies:
+        copy.wait()
 
 
 def near_kernel(
-    inv2_ref, rows_a, rows_b, base_a, base_b, three_b, fold_ref, out_a, out_b, scaled_ref, mixed_ref
+    inv2_ref, rows_a, rows_b, base_a, base_b, face_b, fold_ref, out_a, out_b, left_c, left_d
 ):
-    side = three_b.shape[0]
+    side = face_b.shape[0]
     right = parts_of(rows_a[...])
     scaled = mul_parts(right, parts_of(inv2_ref[...]), ((0,), (0,)))
-    scaled_ref[...] = scaled
+    left_c[:, side:] = -scaled[:, :side]
+    left_d[:, side:] = -scaled[:, side:]
     scaled = parts_of(scaled)
-    mixed_ref[...] = mul_parts(scaled, parts_of(fold_ref[...]))
+    mixed = mul_parts(scaled, parts_of(fold_ref[...]))
+    left_c[:, :side] = mixed
+    left_d[:, :side] = mixed
     out_a[...] = base_a[...] - mul_parts(scaled, right)
     sib = rows_b[...]
-    sib = jnp.concatenate([sib[:side], sib[side:] + three_b[...]], axis=0)
+    sib = jnp.concatenate([sib[:side], sib[side:] + face_b[...]], axis=0)
     out_b[...] = base_b[...] - mul_parts(scaled, parts_of(sib))
 
 
-def cross_kernel(scaled_ref, mixed_ref, two_c, two_d, three_c, out_c, out_d):
-    side = two_c.shape[0]
-    scaled = parts_of(scaled_ref[:, :side])
-    mixed = parts_of(mixed_ref[...])
-    out_c[...] = mul_parts(mixed, parts_of(two_c[...])) - mul_parts(scaled, parts_of(three_c[...]))
-    out_d[...] = mul_parts(mixed, parts_of(two_d[...]))
-
-
-def last_kernel(place_ref, out_a, out_b, out_c, part_d, scaled_ref, three_d, out_any, out_d, sems):
-    side, width = three_d.shape
-    copies = []
-    for k, ref in enumerate((out_a, out_b, out_c, out_d)):
-        lanes = pl.ds(pl.multiple_of(place_ref[k] * width, width), width)
-        copies.append(pltpu.make_async_copy(ref, out_any.at[:, lanes], sems.at[k]))
-    for copy in copies[:3]:
-        copy.start()
-    left = parts_of(scaled_ref[:, side:])
-    out_d[...] = part_d[...] - mul_parts(left, parts_of(three_d[...]))
-    copies[3].start()
-    for copy in copies:
-        copy.wait()
-
-
-def values_kernel(total_own, total_sib, known_ref, inv_ref, inv2_ref, own_ref, sib_ref, out_ref):
-    side = inv_ref.shape[0]
-    face = -mul(inv2_ref[...], jnp.concatenate([total_own[...], total_sib[...]], axis=0))
-    out_ref[:side] = face[:side]
-    inner = (
-        known_ref[...]
-        + mul(own_ref[:side, side:], face[:side])
-        + mul(sib_ref[:side, side:], face[side:])
-    )
-    out_ref[side:] = -mul(inv_ref[...], inner)
-
-
-def call(kernel, outs, args, us, name, specs=None, out_specs=None, scratch=()):
+def cross_kernel(
+    place_ref, fold_any, shift_any, out_a, out_b, left_c, left_d, two_c, three_c, four_c, two_d, three_d,
+    inv2_ref, total_ref, out_any, part_d, map_ref, base_ref, out_c, fold, shift, sems,
+):
+    width = two_c.shape[1]
+    side = width // 2
+    stores = [
+        pltpu.make_async_copy(ref, out_any.at[:, lanes_of(place_ref, k, width)], sems.at[k])
+        for k, ref in enumerate((out_a, out_b, out_c))
+    ]
+    loads = [
+        pltpu.make_async_copy(fold_any, fold, sems.at[3]),
+        pltpu.make_async_copy(shift_any, shift, sems.at[4]),
+    ]
+    start_all(loads)
+    start_all(stores[:2])
+    out_c[...] = mul(left_c[...], jnp.concatenate([two_c[...], three_c[...], four_c[...]], axis=0))
+    stores[2].start()
+    far_d = jnp.concatenate([two_d[...], three_d[...]], axis=0)
+    part_d[...] = mul(left_d[:, : far_d.shape[0]], far_d)
+    wait_all(loads)
+    upper = -inv2_ref[:side]
+    lower = mul_t(fold[...], inv2_ref[...])
+    map_ref[:side] = upper[:, side:]
+    map_ref[side:] = lower[:, side:]
+    total = parts_of(total_ref[...])
+    base_ref[:side] = mul_parts(parts_of(upper[:, :side]), total)
+    base_ref[side:] = mul_parts(parts_of(lower[:, :side]), total) + shift[...]
+    wait_all(stores)
+
+
+def last_kernel(
+    place_ref, in_any, part_d, left_d, four_d, map_ref, base_ref, total_ref,
+    out_any, values_any, out_d, values, sems,
+):
+    tail, width = four_d.shape
+    right = parts_of(four_d[...])
+    values[...] = base_ref[...] + mul(map_ref[...], total_ref[...])
+    values_store = pltpu.make_async_copy(values, values_any, sems.at[4])
+    values_store.start()
+    stores = pieces(out_d, out_any, sems, 0, lanes_of(place_ref, 3, width))
+    rows = width // len(stores)
+    for k, store in enumerate(stores):
+        part = slice(k * rows, (k + 1) * rows)
+        out_d[part] = part_d[part] + mul_parts(parts_of(left_d[part, width - tail :]), right)
+        store.start()
+    wait_all(stores + [values_store])
+
+
+COSTS = {'*': 1000000000, 'own_level': 1500000000, 'own_term': 300000000, 'far_level': 1800000000, 'face_start': 1800000000, 'face_end': 1200000000}
+
+
+def call(kernel, outs, args, us, name, specs=None, out_specs=None, scratch=(), aliases=None):
     return pl.pallas_call(
         kernel,
-        out_shape=[jax.ShapeDtypeStruct(s, f32) for s in outs],
+        out_shape=[
+            pltpu.HBM(s, f32) if spec is HBM else jax.ShapeDtypeStruct(s, f32)
+            for s, spec in zip(outs, out_specs or [VM] * len(outs))
+        ],
         in_specs=specs or [VM] * len(args),
         out_specs=out_specs or [VM] * len(outs),
         scratch_shapes=[pltpu.VMEM(s, f32) if isinstance(s, tuple) else s for s in scratch],
         compiler_params=pltpu.CompilerParams(vmem_limit_bytes=12 * 1024 * 1024),
-        cost_estimate=pl.CostEstimate(flops=int(us * 3e8), bytes_accessed=0, transcendentals=0),
+        cost_estimate=pl.CostEstimate(flops=COSTS.get(name, COSTS["*"]), bytes_accessed=0, transcendentals=0),
+        input_output_aliases=aliases or {},
         name=name,
     )(*args)
 
@@ -363,9 +423,11 @@
     sq, sq2, wide, thin = (side, side), (2 * side, 2 * side), (side, 2 * side), (2 * side, side)
     narrow = (side, ncol)
 
-    one, two, three, more = call(
+    third = 2 * side // 3
+    full = (2 * side, 8 * side)
+    one, two, three, four, face, more = call(
         pack_kernel,
-        [(side + 8, 2 * side), wide, wide, (side + ncol // 2, 2 * side)],
+        [(side + 8, 2 * side)] + [(third, 2 * side)] * 3 + [wide, (side + ncol // 2, 2 * side)],
         tuple(in_hbm(x) for x in (classes, wave_table, raw, data)),
         2,
         "pack",
@@ -389,65 +451,74 @@
     two_z = shifted(two_s, "gy")
     one_zx = shifted(one_z, "gx")
     term, known = call(
-        term_kernel, [narrow] * 2, (fold1, more, more_x, three, data), 1, "own_term"
+        term_kernel, [narrow] * 2, (fold1, more, more_x, face, data), 1, "own_term"
     )
     three_s, more_x, term = after((three, more_x), term)
     three_z = shifted(three_s, "gy")
-    rows_a, rows_b, base_a, base_b = call(
+    rows_a, rows_b, base_a, base_b, fold_h, shift = call(
         rows_kernel,
-        [sq2] * 4,
-        (in_hbm(raw), one, fold1, inv1, more, more_x, three),
+        [sq2] * 4 + [thin, narrow],
+        (in_hbm(raw), one, fold1, inv1, more, more_x, face, known),
         2,
         "pair_rows",
-        specs=[HBM] + [VM] * 6,
-        scratch=[sq2, pltpu.SemaphoreType.DMA(())],
+        specs=[HBM] + [VM] * 7,
+        out_specs=[VM] * 4 + [HBM] * 2,
+        scratch=[sq2, narrow, pltpu.SemaphoreType.DMA((3,))],
     )
     one_zx, rows_a = after((one_zx,), rows_a)
-    three_s, one_zx = after((three,), one_zx)
-    three_x = shifted(three_s, "gx")
+    face_s, one_zx = after((face,), one_zx)
+    face_x = shifted(face_s, "gx")
     fold2, sum2 = call(
         far_kernel, [thin, sq2], (one_z, one_zx, face1), 6, "far_level", scratch=[sq, sq]
     )
     start2, bound2 = call(
         face_start_kernel, [sq2, (8, 128)], (one, sum2), 6, "face_start", scratch=[sq2]
     )
-    term_s, start2 = after((term,), start2)
-    term_z = shifted(term_s, "gy")
     two_z, start2 = after((two_z,), start2)
     two_zx = shifted(two_z, "gx")
     start2, two_z = after((start2,), two_z)
+    four_s, term_s, start2 = after((four, term), start2)
+    four_z = shifted(four_s, "gy")
+    term_z = shifted(term_s, "gy")
+    three_z, start2 = after((three_z,), start2)
+    three_zx = shifted(three_z, "gx")
+    start2, three_z = after((start2,), three_z)
     (inv2,) = call(face_end_kernel, [sq2], (sum2, start2, bound2), 4, "face_end")
-    three_z, inv2 = after((three_z,), inv2)
-    three_zx = shifted(three_z, "gx")
-    out_a, out_b, scaled, mixed = call(
+    out_a, out_b, left_c, left_d = call(
         near_kernel,
-        [sq2, sq2, sq2, thin],
-        (inv2, rows_a, rows_b, base_a, base_b, three_x, fold2),
+        [sq2] * 4,
+        (inv2, rows_a, rows_b, base_a, base_b, face_x, fold2),
         3,
         "near_rows",
     )
-    term_z, scaled = after((term_z,), scaled)
+    four_z, left_c = after((four_z,), left_c)
+    four_zx = shifted(four_z, "gx")
+    term_z, four_z = after((term_z,), four_z)
     total = term + term_z
     total_x = shifted(total, "gx")
-    out_c, part_d = call(
-        cross_kernel, [sq2, sq2], (scaled, mixed, two_z, two_zx, three_z), 2, "cross_rows"
-    )
-    (values,) = call(
-        values_kernel,
-        [(2 * side, ncol)],
-        (total, total_x, known, inv1, inv2, one, one_x),
+    parent, part_d, value_map, value_base = call(
+        cross_kernel,
+        [full, sq2, thin, (2 * side, ncol)],
+        (
+            place, in_hbm(fold_h), in_hbm(shift), out_a, out_b, left_c, left_d, two_z, three_z, four_z,
+            two_zx, three_zx, inv2, total,
+        ),
         2,
-        "values",
-    )
-    (parent,) = call(
+        "cross_rows",
+        specs=[SM, HBM, HBM] + [VM] * 11,
+        out_specs=[HBM, VM, VM, VM],
+        scratch=[sq2, thin, narrow, pltpu.SemaphoreType.DMA((5,))],
+    )
+    parent, values = call(
         last_kernel,
-        [(2 * side, 8 * side)],
-        (place, out_a, out_b, out_c, part_d, scaled, three_zx),
+        [full, (2 * side, ncol)],
+        (place, in_hbm(parent), part_d, left_d, four_zx, value_map, value_base, total_x),
         2,
         "last_rows",
-        specs=[SM] + [VM] * 6,
-        out_specs=[ANY],
-        scratch=[sq2, pltpu.SemaphoreType.DMA((4,))],
+        specs=[SM, HBM] + [VM] * 6,
+        out_specs=[HBM, HBM],
+        scratch=[sq2, (2 * side, ncol), pltpu.SemaphoreType.DMA((5,))],
+        aliases={1: 0},
     )
     return (parent[None, None], values[None, None])
 

time: 65.3 us -> 63.8 us (0.977)
  waiting for transfers between devices: 21.6 us -> 14.3 us
  starting transfers between devices: 15.2 us -> 21.1 us
    ppermute x11 -> x13, waiting for transfers between devices: 21.6 us -> 14.3 us  [shifted(): lax.ppermute(shard, axis, [(i, (i + size // 2) % size) for i in range(siz...]
    ppermute x11 -> x13, starting transfers between devices: 15.2 us -> 21.1 us  [shifted(): lax.ppermute(shard, axis, [(i, (i + size // 2) % size) for i in range(siz...]
    pallas_call x11 -> x10, Pallas kernels: 26.5 us -> 26.3 us  [call(): pl.pallas_call(kernel, out_shape=[pltpu.HBM(s, f32) if spec is HBM else j...]
  transfers between devices with their start and end apart: 11 -> 13, of which waited for: 7 -> 5; matrix products, arithmetic and copies ran while one was open for 0% -> 0% of each run, Pallas kernels for 35% -> 36%
where the time goes in v2:
time: 63.8 us; the launch traced here: 63.6 us
  Pallas kernels  26.3 us (41%)
  starting transfers between devices  21.1 us (33%)
  waiting for transfers between devices  14.3 us (22%)
  between operations  0.91 us (1%)
  local copies, waits for them, and re-layouts  0.82 us (1%)
    pallas_call x10, Pallas kernels, call(): pl.pallas_call(kernel, out_shape=[pltpu.HBM(s, f32) if spec is HBM else j...  26.3 us
    ppermute x13, starting transfers between devices, shifted(): lax.ppermute(shard, axis, [(i, (i + size // 2) % size) for i in range(siz...  21.1 us
    ppermute x13, waiting for transfers between devices, shifted(): lax.ppermute(shard, axis, [(i, (i + size // 2) % size) for i in range(siz...  14.3 us
  transfers between devices with their start and end apart: 13, of which 5 were waited for; matrix products, arithmetic and copies ran while one was open for 0% of the time, Pallas kernels for 36%

profile of v2, /device:TPU:0, one launch (start us, length us, event | category | flops | bytes accessed | tf_op | source)
XLA Modules:
  0.0 63.6 jit_solution(13240199140644554409)
XLA Ops:
  0.6 1.7 %pack.1 = (f32[200,384]{1,0:T(8,128)S(1)}, f32[128,384]{1,0:T(8,128)S(1)}, f32[128,384]{1,0:T(8,128)S(1)}, f32[128,384]{1,0:T(8,128)S(1)}, f32[192,384]{1,0:T(8,128)S(1)}, /*index=5*/f32[256,384]{1,0:T(8,128)S(1)}) custom-call(s32[12]{0:T(128)} %bitcast.15, f32[8]{0:T(128)} %table_any.1, f32[768,768]{1,0:T(8,128)} %bitcast.11, f32[384,128]{1,0:T(8,128)} %bitcast.9), custom_call_target="tpu_custom_call" | custom-call | flops 1000000000 | tf_op jit(solution)/shard_map/pack/pallas_call | solution.py:385
  2.3 3.0 %collective-permute-start = (f32[200,384]{1,0:T(8,128)S(1)}, f32[200,384]{1,0:T(8,128)S(1)}, u32[]{:S(2)}, u32[]{:S(2)}) collective-permute-start(f32[200,384]{1,0:T(8,128)S(1)} %get-tuple-element.60.own_ref.one_ref), channel_id=1, source_target_pairs={{0,16},{8,24},{16,0},{24,8},{1,17},{9,25},{17,1},{25,9},{2,18},{10... | collective-permute-start | bytes 921608 | tf_op jit(solution)/shard_map/ppermute | solution.py:21
  5.3 2.6 %collective-permute-start.1 = (f32[200,384]{1,0:T(8,128)S(1)}, f32[200,384]{1,0:T(8,128)S(1)}, u32[]{:S(2)}, u32[]{:S(2)}) collective-permute-start(f32[200,384]{1,0:T(8,128)S(1)} %get-tuple-element.60.own_ref.one_ref), channel_id=1, source_target_pairs={{0,4},{1,5},{2,6},{3,7},{4,0},{5,1},{6,2},{7,3},{8,12},{9,13},{10,... | collective-permute-start | bytes 921608 | tf_op jit(solution)/shard_map/ppermute | solution.py:21
  7.9 4.7 %collective-permute-done.sib_ref = f32[200,384]{1,0:T(8,128)S(1)} collective-permute-done((f32[200,384]{1,0:T(8,128)S(1)}, f32[200,384]{1,0:T(8,128)S(1)}, u32[]{:S(2)}, u32[]{:S(2)}) %collective-permute-start) | collective-permute-done | bytes 307232 | tf_op jit(solution)/shard_map/ppermute | solution.py:21
  12.6 1.7 %collective-permute-start.2 = (f32[256,384]{1,0:T(8,128)S(1)}, f32[256,384]{1,0:T(8,128)S(1)}, u32[]{:S(2)}, u32[]{:S(2)}) collective-permute-start(f32[256,384]{1,0:T(8,128)S(1)} %get-tuple-element.68.more_a), channel_id=1, source_target_pairs={{0,16},{8,24},{16,0},{24,8},{1,17},{9,25},{17,1},{25,9},{2,18},{10... | collective-permute-start | bytes 1179656 | tf_op jit(solution)/shard_map/ppermute | solution.py:21
  14.3 3.6 %own_level.1 = (f32[192,192]{1,0:T(8,128)S(1)}, f32[384,192]{1,0:T(8,128)S(1)}, f32[384,384]{1,0:T(8,128)S(1)}) custom-call(f32[200,384]{1,0:T(8,128)S(1)} %get-tuple-element.60.own_ref.one_ref, f32[200,384]{1,0:T(8,128)S(1)} %collective-permute-done.sib_ref), custom_call_target="tpu_custom_call" | custom-call | flops 1500000000 | tf_op jit(solution)/shard_map/own_level/pallas_call | solution.py:385
  17.9 0.8 %copy-done.1 = f32[384,384]{1,0:T(8,128)} copy-done((f32[384,384]{1,0:T(8,128)}, f32[384,384]{1,0:T(8,128)S(1)}, u32[]{:S(2)}) %copy-start.1) | copy-done | bytes 589848
  18.7 2.8 %collective-permute-done.1.own_ref = f32[200,384]{1,0:T(8,128)S(1)} collective-permute-done((f32[200,384]{1,0:T(8,128)S(1)}, f32[200,384]{1,0:T(8,128)S(1)}, u32[]{:S(2)}, u32[]{:S(2)}) %collective-permute-start.1) | collective-permute-done | bytes 307232 | tf_op jit(solution)/shard_map/ppermute | solution.py:21
  22.0 0.9 %collective-permute-done.2.more_b = f32[256,384]{1,0:T(8,128)S(1)} collective-permute-done((f32[256,384]{1,0:T(8,128)S(1)}, f32[256,384]{1,0:T(8,128)S(1)}, u32[]{:S(2)}, u32[]{:S(2)}) %collective-permute-start.2) | collective-permute-done | bytes 393248 | tf_op jit(solution)/shard_map/ppermute | solution.py:21
  23.3 4.7 %collective-permute-start.4 = (f32[128,384]{1,0:T(8,128)S(1)}, f32[128,384]{1,0:T(8,128)S(1)}, u32[]{:S(2)}, u32[]{:S(2)}) collective-permute-start(f32[128,384]{1,0:T(8,128)S(1)} %get-tuple-element.81), channel_id=1, source_target_pairs={{0,4},{1,5},{2,6},{3,7},{4,0},{5,1},{6,2},{7,3},{8,12},{9,13},{10,... | collective-permute-start | bytes 589832 | tf_op jit(solution)/shard_map/ppermute | solution.py:21
  27.9 2.4 %pair_rows.1 = (f32[384,384]{1,0:T(8,128)S(1)}, f32[384,384]{1,0:T(8,128)S(1)}, f32[384,384]{1,0:T(8,128)S(1)}, f32[384,384]{1,0:T(8,128)S(1)}, f32[384,192]{1,0:T(8,128)}, /*index=5*/f32[192,128]{1,0:T(8,128)}) custom-call(f32[768,768]{1,0:T(8,128)} %bitcast.12, f32[200,384]{1,0:T(8,128)S(1)} %get-tuple-element.60.own_ref.one_ref, ...), custom_call_target="tpu_custom_call" | custom-call | flops 1000000000 | tf_op jit(solution)/shard_map/pair_rows/pallas_call | solution.py:385
  30.4 1.6 %collective-permute-start.6 = (f32[192,384]{1,0:T(8,128)S(1)}, f32[192,384]{1,0:T(8,128)S(1)}, u32[]{:S(2)}, u32[]{:S(2)}) collective-permute-start(f32[192,384]{1,0:T(8,128)S(1)} %get-tuple-element.98.three_ref), channel_id=1, source_target_pairs={{0,16},{8,24},{16,0},{24,8},{1,17},{9,25},{17,1},{25,9},{2,18},{10... | collective-permute-start | bytes 884744 | tf_op jit(solution)/shard_map/ppermute | solution.py:21
  31.9 3.5 %far_level.1 = (f32[384,192]{1,0:T(8,128)S(1)}, f32[384,384]{1,0:T(8,128)S(1)}) custom-call(f32[200,384]{1,0:T(8,128)S(1)} %collective-permute-done.1.own_ref, f32[200,384]{1,0:T(8,128)S(1)} %collective-permute-done.3.sib_ref, f32[384,384]{1,0:T(8,128)S(1)} %copy-done.2), custom_call_target="tpu_custom_call" | custom-call | flops 1800000000 | tf_op jit(solution)/shard_map/far_level/pallas_call | solution.py:385
  35.5 4.9 %face_start.1 = (f32[384,384]{1,0:T(8,128)S(1)}, f32[8,128]{1,0:T(8,128)S(1)}) custom-call(f32[200,384]{1,0:T(8,128)S(1)} %get-tuple-element.60.own_ref.one_ref, f32[384,384]{1,0:T(8,128)S(1)} %get-tuple-element.80.sum_ref), custom_call_target="tpu_custom_call" | custom-call | flops 1800000000 | tf_op jit(solution)/shard_map/face_start/pallas_call | solution.py:385
  41.0 1.6 %collective-permute-start.8 = (f32[192,128]{1,0:T(8,128)S(1)}, f32[192,128]{1,0:T(8,128)S(1)}, u32[]{:S(2)}, u32[]{:S(2)}) collective-permute-start(f32[192,128]{1,0:T(8,128)S(1)} %get-tuple-element.108), channel_id=1, source_target_pairs={{0,4},{1,5},{2,6},{3,7},{4,0},{5,1},{6,2},{7,3},{8,12},{9,13},{10,... | collective-permute-start | bytes 294920 | tf_op jit(solution)/shard_map/ppermute | solution.py:21
  42.5 1.4 %collective-permute-start.7 = (f32[128,384]{1,0:T(8,128)S(1)}, f32[128,384]{1,0:T(8,128)S(1)}, u32[]{:S(2)}, u32[]{:S(2)}) collective-permute-start(f32[128,384]{1,0:T(8,128)S(1)} %get-tuple-element.102), channel_id=1, source_target_pairs={{0,4},{1,5},{2,6},{3,7},{4,0},{5,1},{6,2},{7,3},{8,12},{9,13},{10,... | collective-permute-start | bytes 589832 | tf_op jit(solution)/shard_map/ppermute | solution.py:21
  43.9 1.5 %collective-permute-start.10 = (f32[128,384]{1,0:T(8,128)S(1)}, f32[128,384]{1,0:T(8,128)S(1)}, u32[]{:S(2)}, u32[]{:S(2)}) collective-permute-start(f32[128,384]{1,0:T(8,128)S(1)} %collective-permute-done.4.three_c), channel_id=1, source_target_pairs={{0,16},{8,24},{16,0},{24,8},{1,17},{9,25},{17,1},{25,9},{2,18},{10... | collective-permute-start | bytes 589832 | tf_op jit(solution)/shard_map/ppermute | solution.py:21
  45.4 2.9 %face_end.1.inv2_ref = f32[384,384]{1,0:T(8,128)S(1)} custom-call(f32[384,384]{1,0:T(8,128)S(1)} %get-tuple-element.80.sum_ref, f32[384,384]{1,0:T(8,128)S(1)} %get-tuple-element.92.start_ref, f32[8,128]{1,0:T(8,128)S(1)} %get-tuple-element.93.bound_ref), custom_call_target="tpu_custom_call" | custom-call | flops 1200000000 | tf_op jit(solution)/shard_map/face_end/pallas_call | solution.py:385
  48.3 2.3 %near_rows.1 = (f32[384,384]{1,0:T(8,128)S(1)}, f32[384,384]{1,0:T(8,128)S(1)}, f32[384,384]{1,0:T(8,128)S(1)}, f32[384,384]{1,0:T(8,128)S(1)}) custom-call(f32[384,384]{1,0:T(8,128)S(1)} %face_end.1.inv2_ref, f32[384,384]{1,0:T(8,128)S(1)} %get-tuple-element.94.rows_a, f32[384,384]{1,0:T(8,128)S(1)} %get-tuple-element.95.rows_b, ...), custom_call_target="tpu_custom_call" | custom-call | flops 1000000000 | tf_op jit(solution)/shard_map/near_rows/pallas_call | solution.py:385
  50.6 4.2 %collective-permute-done.7.four_c = f32[128,384]{1,0:T(8,128)S(1)} collective-permute-done((f32[128,384]{1,0:T(8,128)S(1)}, f32[128,384]{1,0:T(8,128)S(1)}, u32[]{:S(2)}, u32[]{:S(2)}) %collective-permute-start.7) | collective-permute-done | bytes 196640 | tf_op jit(solution)/shard_map/ppermute | solution.py:21
  54.8 1.5 %collective-permute-start.11 = (f32[128,384]{1,0:T(8,128)S(1)}, f32[128,384]{1,0:T(8,128)S(1)}, u32[]{:S(2)}, u32[]{:S(2)}) collective-permute-start(f32[128,384]{1,0:T(8,128)S(1)} %collective-permute-done.7.four_c), channel_id=1, source_target_pairs={{0,16},{8,24},{16,0},{24,8},{1,17},{9,25},{17,1},{25,9},{2,18},{10... | collective-permute-start | bytes 589832 | tf_op jit(solution)/shard_map/ppermute | solution.py:21
  57.0 2.8 %cross_rows.1 = (f32[384,1536]{1,0:T(8,128)}, f32[384,384]{1,0:T(8,128)S(1)}, f32[384,192]{1,0:T(8,128)S(1)}, f32[384,128]{1,0:T(8,128)S(1)}) custom-call(s32[4]{0:T(128)S(1)} %pad_add_fusion.place_ref, f32[384,192]{1,0:T(8,128)} %get-tuple-element.73.fold_any, f32[192,128]{1,0:T(8,128)} %get-tuple-element.74.shift_any, ...), custom_call_target="tpu_custom_call" | custom-call | flops 1000000000 | tf_op jit(solution)/shard_map/cross_rows/pallas_call | solution.py:385
  59.8 1.8 %collective-permute-done.12.total_ref = f32[192,128]{1,0:T(8,128)S(1)} collective-permute-done((f32[192,128]{1,0:T(8,128)S(1)}, f32[192,128]{1,0:T(8,128)S(1)}, u32[]{:S(2)}, u32[]{:S(2)}) %collective-permute-start.12) | collective-permute-done | bytes 98336 | tf_op jit(solution)/shard_map/ppermute | solution.py:21
  61.6 1.9 %last_rows.1 = (f32[384,1536]{1,0:T(8,128)}, f32[384,128]{1,0:T(8,128)}) custom-call(s32[4]{0:T(128)S(1)} %pad_add_fusion.place_ref, f32[384,1536]{1,0:T(8,128)} %get-tuple-element.112.in_any, f32[384,384]{1,0:T(8,128)S(1)} %get-tuple-element.113.part_d, f32[384,384]{1,0:T(8,128)S(1)} %get-tuple-element.105.left_d, ...), custom_call_target="tpu_custom_call", output_to_operand_aliasing={{0}: (1, {})} | custom-call | flops 1000000000 | tf_op jit(solution)/shard_map/last_rows/pallas_call | solution.py:385
  (20 shorter events, 2.2 us)
Async XLA Ops:
  2.3 10.3 %collective-permute-start = (f32[200,384]{1,0:T(8,128)S(1)}, f32[200,384]{1,0:T(8,128)S(1)}, u32[]{:S(2)}, u32[]{:S(2)}) collective-permute-start(f32[200,384]{1,0:T(8,128)S(1)} %get-tuple-element.60.own_ref.one_ref), channel_id=1, source_target_pairs={{0,16},{8,24},{16,0},{24,8},{1,17},{9,25},{17,1},{25,9},{2,18},{10... | collective-permute-start | bytes 921608 | tf_op jit(solution)/shard_map/ppermute | solution.py:21
  5.3 16.2 %collective-permute-start.1 = (f32[200,384]{1,0:T(8,128)S(1)}, f32[200,384]{1,0:T(8,128)S(1)}, u32[]{:S(2)}, u32[]{:S(2)}) collective-permute-start(f32[200,384]{1,0:T(8,128)S(1)} %get-tuple-element.60.own_ref.one_ref), channel_id=1, source_target_pairs={{0,4},{1,5},{2,6},{3,7},{4,0},{5,1},{6,2},{7,3},{8,12},{9,13},{10,... | collective-permute-start | bytes 921608 | tf_op jit(solution)/shard_map/ppermute | solution.py:21
  12.6 10.3 %copy-start = (f32[1,1,384,128]{3,2,1,0:T(8,128)S(1)}, f32[1,1,384,128]{3,2,1,0:T(8,128)}, u32[]{:S(2)}) copy-start(f32[1,1,384,128]{3,2,1,0:T(8,128)} %param.7) | copy-start | bytes 589828
  12.6 10.3 %collective-permute-start.2 = (f32[256,384]{1,0:T(8,128)S(1)}, f32[256,384]{1,0:T(8,128)S(1)}, u32[]{:S(2)}, u32[]{:S(2)}) collective-permute-start(f32[256,384]{1,0:T(8,128)S(1)} %get-tuple-element.68.more_a), channel_id=1, source_target_pairs={{0,16},{8,24},{16,0},{24,8},{1,17},{9,25},{17,1},{25,9},{2,18},{10... | collective-permute-start | bytes 1179656 | tf_op jit(solution)/shard_map/ppermute | solution.py:21
  17.9 0.8 %copy-start.1 = (f32[384,384]{1,0:T(8,128)}, f32[384,384]{1,0:T(8,128)S(1)}, u32[]{:S(2)}) copy-start(f32[384,384]{1,0:T(8,128)S(1)} %get-tuple-element.79.near_ref) | copy-start | bytes 1769476
  21.5 8.8 %collective-permute-start.3 = (f32[200,384]{1,0:T(8,128)S(1)}, f32[200,384]{1,0:T(8,128)S(1)}, u32[]{:S(2)}, u32[]{:S(2)}) collective-permute-start(f32[200,384]{1,0:T(8,128)S(1)} %collective-permute-done.1.own_ref), channel_id=1, source_target_pairs={{0,16},{8,24},{16,0},{24,8},{1,17},{9,25},{17,1},{25,9},{2,18},{10... | collective-permute-start | bytes 921608 | tf_op jit(solution)/shard_map/ppermute | solution.py:21
  22.0 18.4 %collective-permute-start.5 = (f32[128,384]{1,0:T(8,128)S(1)}, f32[128,384]{1,0:T(8,128)S(1)}, u32[]{:S(2)}, u32[]{:S(2)}) collective-permute-start(f32[128,384]{1,0:T(8,128)S(1)} %get-tuple-element.84), channel_id=1, source_target_pairs={{0,4},{1,5},{2,6},{3,7},{4,0},{5,1},{6,2},{7,3},{8,12},{9,13},{10,... | collective-permute-start | bytes 589832 | tf_op jit(solution)/shard_map/ppermute | solution.py:21
  23.3 8.7 %copy-start.2 = (f32[384,384]{1,0:T(8,128)S(1)}, f32[384,384]{1,0:T(8,128)}, u32[]{:S(2)}) copy-start(f32[384,384]{1,0:T(8,128)} %copy-done.1) | copy-start | bytes 1769476
  23.3 20.6 %collective-permute-start.4 = (f32[128,384]{1,0:T(8,128)S(1)}, f32[128,384]{1,0:T(8,128)S(1)}, u32[]{:S(2)}, u32[]{:S(2)}) collective-permute-start(f32[128,384]{1,0:T(8,128)S(1)} %get-tuple-element.81), channel_id=1, source_target_pairs={{0,4},{1,5},{2,6},{3,7},{4,0},{5,1},{6,2},{7,3},{8,12},{9,13},{10,... | collective-permute-start | bytes 589832 | tf_op jit(solution)/shard_map/ppermute | solution.py:21
  30.4 17.9 %collective-permute-start.6 = (f32[192,384]{1,0:T(8,128)S(1)}, f32[192,384]{1,0:T(8,128)S(1)}, u32[]{:S(2)}, u32[]{:S(2)}) collective-permute-start(f32[192,384]{1,0:T(8,128)S(1)} %get-tuple-element.98.three_ref), channel_id=1, source_target_pairs={{0,16},{8,24},{16,0},{24,8},{1,17},{9,25},{17,1},{25,9},{2,18},{10... | collective-permute-start | bytes 884744 | tf_op jit(solution)/shard_map/ppermute | solution.py:21
  40.4 16.6 %collective-permute-start.9 = (f32[128,384]{1,0:T(8,128)S(1)}, f32[128,384]{1,0:T(8,128)S(1)}, u32[]{:S(2)}, u32[]{:S(2)}) collective-permute-start(f32[128,384]{1,0:T(8,128)S(1)} %collective-permute-done.5.two_c), channel_id=1, source_target_pairs={{0,16},{8,24},{16,0},{24,8},{1,17},{9,25},{17,1},{25,9},{2,18},{10... | collective-permute-start | bytes 589832 | tf_op jit(solution)/shard_map/ppermute | solution.py:21
  41.0 15.3 %collective-permute-start.8 = (f32[192,128]{1,0:T(8,128)S(1)}, f32[192,128]{1,0:T(8,128)S(1)}, u32[]{:S(2)}, u32[]{:S(2)}) collective-permute-start(f32[192,128]{1,0:T(8,128)S(1)} %get-tuple-element.108), channel_id=1, source_target_pairs={{0,4},{1,5},{2,6},{3,7},{4,0},{5,1},{6,2},{7,3},{8,12},{9,13},{10,... | collective-permute-start | bytes 294920 | tf_op jit(solution)/shard_map/ppermute | solution.py:21
  42.5 12.3 %collective-permute-start.7 = (f32[128,384]{1,0:T(8,128)S(1)}, f32[128,384]{1,0:T(8,128)S(1)}, u32[]{:S(2)}, u32[]{:S(2)}) collective-permute-start(f32[128,384]{1,0:T(8,128)S(1)} %get-tuple-element.102), channel_id=1, source_target_pairs={{0,4},{1,5},{2,6},{3,7},{4,0},{5,1},{6,2},{7,3},{8,12},{9,13},{10,... | collective-permute-start | bytes 589832 | tf_op jit(solution)/shard_map/ppermute | solution.py:21
  43.9 13.1 %collective-permute-start.10 = (f32[128,384]{1,0:T(8,128)S(1)}, f32[128,384]{1,0:T(8,128)S(1)}, u32[]{:S(2)}, u32[]{:S(2)}) collective-permute-start(f32[128,384]{1,0:T(8,128)S(1)} %collective-permute-done.4.three_c), channel_id=1, source_target_pairs={{0,16},{8,24},{16,0},{24,8},{1,17},{9,25},{17,1},{25,9},{2,18},{10... | collective-permute-start | bytes 589832 | tf_op jit(solution)/shard_map/ppermute | solution.py:21
  54.8 6.7 %collective-permute-start.11 = (f32[128,384]{1,0:T(8,128)S(1)}, f32[128,384]{1,0:T(8,128)S(1)}, u32[]{:S(2)}, u32[]{:S(2)}) collective-permute-start(f32[128,384]{1,0:T(8,128)S(1)} %collective-permute-done.7.four_c), channel_id=1, source_target_pairs={{0,16},{8,24},{16,0},{24,8},{1,17},{9,25},{17,1},{25,9},{2,18},{10... | collective-permute-start | bytes 589832 | tf_op jit(solution)/shard_map/ppermute | solution.py:21
  56.3 5.2 %collective-permute-start.12 = (f32[192,128]{1,0:T(8,128)S(1)}, f32[192,128]{1,0:T(8,128)S(1)}, u32[]{:S(2)}, u32[]{:S(2)}) collective-permute-start(f32[192,128]{1,0:T(8,128)S(1)} %add.17.total_ref), channel_id=1, source_target_pairs={{0,16},{8,24},{16,0},{24,8},{1,17},{9,25},{17,1},{25,9},{2,18},{10... | collective-permute-start | bytes 294920 | tf_op jit(solution)/shard_map/ppermute | solution.py:21

commit v3 on v2

--- a/solution.py
+++ b/solution.py
@@ -129,10 +129,7 @@
     invert_end(mat, invert_start(mat, least, inv_ref, res_ref), inv_ref)
 
 
-def pack_kernel(
-    class_any, table_any, raw_any, data_any, one_ref, two_ref, three_ref, four_ref, face_ref, more_ref,
-    classes, table, raw, data, sems,
-):
+def pack_kernel(class_any, table_any, raw_any, one_ref, classes, table, raw, sems):
     bound = raw_any.shape[0]
     side = bound // 4
     blk = bound // class_any.shape[0]
@@ -140,14 +137,13 @@
     copies = [
         pltpu.make_async_copy(class_any, classes, sems.at[0]),
         pltpu.make_async_copy(table_any, table, sems.at[1]),
-        pltpu.make_async_copy(raw_any.at[pl.ds(2 * side, 2 * side)], raw, sems.at[2]),
-        pltpu.make_async_copy(data_any, data, sems.at[3]),
+        pltpu.make_async_copy(
+            raw_any.at[pl.ds(2 * side, 2 * side), pl.ds(2 * side, 2 * side)], raw, sems.at[2]
+        ),
     ]
-    for copy in copies:
-        copy.start()
+    start_all(copies)
     row, col = rows_of(shape), cols_of(shape)
-    for copy in copies:
-        copy.wait()
+    wait_all(copies)
     least = table[0]
     for k in range(1, table.shape[0]):
         least = jnp.minimum(least, table[k])
@@ -161,23 +157,32 @@
     def with_diagonal(block, start):
         return block + jnp.where(row == col, level_of(row, start // blk, side // blk), 0.0)
 
-    face = with_diagonal(raw[:side, 2 * side : 3 * side], 2 * side)
-    inner = with_diagonal(raw[side:, 3 * side :], 3 * side)
+    face = with_diagonal(raw[:side, :side], 2 * side)
+    inner = with_diagonal(raw[side:, side:], 3 * side)
     one_ref[:side, :side] = jnp.where(row <= col, inner, face)
-    one_ref[:side, side:] = raw[side:, 2 * side : 3 * side]
+    one_ref[:side, side:] = raw[side:, :side]
     one_ref[side : side + 8, :] = jnp.zeros((8, 2 * side), f32)
     one_ref[side : side + 1, :side] = jnp.sum(
         jnp.where(row == col, face, 0.0), axis=0, keepdims=True
     )
     one_ref[side + 1 : side + 2, :] = level_of(cols_of((1, 2 * side)), 0, 2 * side // blk)
     one_ref[side + 2 : side + 3, :] = jnp.zeros((1, 2 * side), f32) + 2.0 * (LEAST + least)
-    inner_out = raw[side:, : 2 * side]
-    face_ref[...] = raw[:side, : 2 * side]
-    outer = jnp.concatenate([inner_out, raw[:side, : 2 * side]], axis=0)
-    cut = 0
-    for ref in (two_ref, three_ref, four_ref):
-        ref[...] = outer[cut : cut + ref.shape[0]]
-        cut = cut + ref.shape[0]
+
+
+def outer_kernel(raw_any, data_any, two_ref, three_ref, four_ref, face_ref, more_ref, raw, data, sems):
+    side = raw.shape[0] // 2
+    copies = [
+        pltpu.make_async_copy(raw_any.at[pl.ds(2 * side, 2 * side), pl.ds(0, 2 * side)], raw, sems.at[0]),
+        pltpu.make_async_copy(data_any, data, sems.at[1]),
+    ]
+    start_all(copies)
+    wait_all(copies)
+    inner_out = raw[side:]
+    face_ref[...] = raw[:side]
+    outer = jnp.concatenate([inner_out, raw[:side]], axis=0)
+    third = two_ref.shape[0]
+    for k, ref in enumerate((two_ref, three_ref, four_ref)):
+        ref[...] = outer[k * third : (k + 1) * third]
     more_ref[:side] = inner_out
     known = mul(inner_out, data[...])
     rows, ncol = more_ref.shape[0] - side, data.shape[1]
@@ -425,20 +430,28 @@
 
     third = 2 * side // 3
     full = (2 * side, 8 * side)
-    one, two, three, four, face, more = call(
+    (one,) = call(
         pack_kernel,
-        [(side + 8, 2 * side)] + [(third, 2 * side)] * 3 + [wide, (side + ncol // 2, 2 * side)],
-        tuple(in_hbm(x) for x in (classes, wave_table, raw, data)),
-        2,
+        [(side + 8, 2 * side)],
+        tuple(in_hbm(x) for x in (classes, wave_table, raw)),
+        1,
         "pack",
-        specs=[HBM] * 4,
+        specs=[HBM] * 3,
         scratch=[
             pltpu.SMEM(classes.shape, jnp.int32),
             pltpu.SMEM(wave_table.shape, f32),
-            (2 * side, bound),
-            data.shape,
-            pltpu.SemaphoreType.DMA((4,)),
+            sq2,
+            pltpu.SemaphoreType.DMA((3,)),
         ],
+    )
+    two, three, four, face, more = call(
+        outer_kernel,
+        [(third, 2 * side)] * 3 + [wide, (side + ncol // 2, 2 * side)],
+        tuple(in_hbm(x) for x in (raw, data)),
+        1,
+        "outer",
+        specs=[HBM] * 2,
+        scratch=[sq2, data.shape, pltpu.SemaphoreType.DMA((2,))],
     )
     one_z = shifted(one, "gy")
     one_x = shifted(one, "gx")
@@ -491,11 +504,11 @@
         3,
         "near_rows",
     )
-    four_z, left_c = after((four_z,), left_c)
-    four_zx = shifted(four_z, "gx")
-    term_z, four_z = after((term_z,), four_z)
+    term_z, left_c = after((term_z,), left_c)
     total = term + term_z
     total_x = shifted(total, "gx")
+    four_z, total = after((four_z,), total)
+    four_zx = shifted(four_z, "gx")
     parent, part_d, value_map, value_base = call(
         cross_kernel,
         [full, sq2, thin, (2 * side, ncol)],

time: 63.8 us -> 62.4 us (0.978)
  waiting for transfers between devices: 14.3 us -> 10.8 us
  Pallas kernels: 26.3 us -> 27.4 us
  starting transfers between devices: 21.1 us -> 22.1 us
    ppermute x13, waiting for transfers between devices: 14.3 us -> 10.8 us  [shifted(): lax.ppermute(shard, axis, [(i, (i + size // 2) % size) for i in range(siz...]
    pallas_call x10 -> x11, Pallas kernels: 26.3 us -> 27.4 us  [call(): pl.pallas_call(kernel, out_shape=[pltpu.HBM(s, f32) if spec is HBM else j...]
    ppermute x13, starting transfers between devices: 21.1 us -> 22.1 us  [shifted(): lax.ppermute(shard, axis, [(i, (i + size // 2) % size) for i in range(siz...]
  transfers between devices with their start and end apart: 13 -> 13, of which waited for: 5 -> 6; matrix products, arithmetic and copies ran while one was open for 0% -> 0% of each run, Pallas kernels for 36% -> 39%
where the time goes in v3:
time: 62.4 us; the launch traced here: 62.2 us
  Pallas kernels  27.4 us (44%)
  starting transfers between devices  22.1 us (35%)
  waiting for transfers between devices  10.8 us (17%)
  between operations  0.93 us (1%)
  local copies, waits for them, and re-layouts  0.82 us (1%)
    pallas_call x11, Pallas kernels, call(): pl.pallas_call(kernel, out_shape=[pltpu.HBM(s, f32) if spec is HBM else j...  27.4 us
    ppermute x13, starting transfers between devices, shifted(): lax.ppermute(shard, axis, [(i, (i + size // 2) % size) for i in range(siz...  22.1 us
    ppermute x13, waiting for transfers between devices, shifted(): lax.ppermute(shard, axis, [(i, (i + size // 2) % size) for i in range(siz...  10.8 us
  transfers between devices with their start and end apart: 13, of which 6 were waited for; matrix products, arithmetic and copies ran while one was open for 0% of the time, Pallas kernels for 39%

profile of v3, /device:TPU:0, one launch (start us, length us, event | category | flops | bytes accessed | tf_op | source)
XLA Modules:
  0.0 62.2 jit_solution(12776132166119544778)
XLA Ops:
  0.6 1.3 %pack.1.own_ref.one_ref = f32[200,384]{1,0:T(8,128)S(1)} custom-call(s32[12]{0:T(128)} %bitcast.16, f32[8]{0:T(128)} %table_any.1, f32[768,768]{1,0:T(8,128)} %bitcast.11), custom_call_target="tpu_custom_call" | custom-call | flops 1000000000 | tf_op jit(solution)/shard_map/pack/pallas_call | solution.py:390
  2.0 3.0 %collective-permute-start = (f32[200,384]{1,0:T(8,128)S(1)}, f32[200,384]{1,0:T(8,128)S(1)}, u32[]{:S(2)}, u32[]{:S(2)}) collective-permute-start(f32[200,384]{1,0:T(8,128)S(1)} %pack.1.own_ref.one_ref), channel_id=1, source_target_pairs={{0,16},{8,24},{16,0},{24,8},{1,17},{9,25},{17,1},{25,9},{2,18},{10... | collective-permute-start | bytes 921608 | tf_op jit(solution)/shard_map/ppermute | solution.py:21
  5.0 2.6 %collective-permute-start.1 = (f32[200,384]{1,0:T(8,128)S(1)}, f32[200,384]{1,0:T(8,128)S(1)}, u32[]{:S(2)}, u32[]{:S(2)}) collective-permute-start(f32[200,384]{1,0:T(8,128)S(1)} %pack.1.own_ref.one_ref), channel_id=1, source_target_pairs={{0,4},{1,5},{2,6},{3,7},{4,0},{5,1},{6,2},{7,3},{8,12},{9,13},{10,... | collective-permute-start | bytes 921608 | tf_op jit(solution)/shard_map/ppermute | solution.py:21
  7.6 1.5 %outer.1 = (f32[128,384]{1,0:T(8,128)S(1)}, f32[128,384]{1,0:T(8,128)S(1)}, f32[128,384]{1,0:T(8,128)S(1)}, f32[192,384]{1,0:T(8,128)S(1)}, f32[256,384]{1,0:T(8,128)S(1)}) custom-call(f32[768,768]{1,0:T(8,128)} %bitcast.12, f32[384,128]{1,0:T(8,128)} %bitcast.9), custom_call_target="tpu_custom_call" | custom-call | flops 1000000000 | tf_op jit(solution)/shard_map/outer/pallas_call | solution.py:390
  9.0 3.2 %collective-permute-done.sib_ref = f32[200,384]{1,0:T(8,128)S(1)} collective-permute-done((f32[200,384]{1,0:T(8,128)S(1)}, f32[200,384]{1,0:T(8,128)S(1)}, u32[]{:S(2)}, u32[]{:S(2)}) %collective-permute-start) | collective-permute-done | bytes 307232 | tf_op jit(solution)/shard_map/ppermute | solution.py:21
  12.2 1.7 %collective-permute-start.2 = (f32[256,384]{1,0:T(8,128)S(1)}, f32[256,384]{1,0:T(8,128)S(1)}, u32[]{:S(2)}, u32[]{:S(2)}) collective-permute-start(f32[256,384]{1,0:T(8,128)S(1)} %get-tuple-element.66.more_a), channel_id=1, source_target_pairs={{0,16},{8,24},{16,0},{24,8},{1,17},{9,25},{17,1},{25,9},{2,18},{10... | collective-permute-start | bytes 1179656 | tf_op jit(solution)/shard_map/ppermute | solution.py:21
  14.0 3.6 %own_level.1 = (f32[192,192]{1,0:T(8,128)S(1)}, f32[384,192]{1,0:T(8,128)S(1)}, f32[384,384]{1,0:T(8,128)S(1)}) custom-call(f32[200,384]{1,0:T(8,128)S(1)} %pack.1.own_ref.one_ref, f32[200,384]{1,0:T(8,128)S(1)} %collective-permute-done.sib_ref), custom_call_target="tpu_custom_call" | custom-call | flops 1500000000 | tf_op jit(solution)/shard_map/own_level/pallas_call | solution.py:390
  18.4 2.8 %collective-permute-done.1.own_ref = f32[200,384]{1,0:T(8,128)S(1)} collective-permute-done((f32[200,384]{1,0:T(8,128)S(1)}, f32[200,384]{1,0:T(8,128)S(1)}, u32[]{:S(2)}, u32[]{:S(2)}) %collective-permute-start.1) | collective-permute-done | bytes 307232 | tf_op jit(solution)/shard_map/ppermute | solution.py:21
  22.9 4.7 %collective-permute-start.4 = (f32[128,384]{1,0:T(8,128)S(1)}, f32[128,384]{1,0:T(8,128)S(1)}, u32[]{:S(2)}, u32[]{:S(2)}) collective-permute-start(f32[128,384]{1,0:T(8,128)S(1)} %get-tuple-element.79), channel_id=1, source_target_pairs={{0,4},{1,5},{2,6},{3,7},{4,0},{5,1},{6,2},{7,3},{8,12},{9,13},{10,... | collective-permute-start | bytes 589832 | tf_op jit(solution)/shard_map/ppermute | solution.py:21
  27.6 2.4 %pair_rows.1 = (f32[384,384]{1,0:T(8,128)S(1)}, f32[384,384]{1,0:T(8,128)S(1)}, f32[384,384]{1,0:T(8,128)S(1)}, f32[384,384]{1,0:T(8,128)S(1)}, f32[384,192]{1,0:T(8,128)}, /*index=5*/f32[192,128]{1,0:T(8,128)}) custom-call(f32[768,768]{1,0:T(8,128)} %bitcast.13, f32[200,384]{1,0:T(8,128)S(1)} %pack.1.own_ref.one_ref, ...), custom_call_target="tpu_custom_call" | custom-call | flops 1000000000 | tf_op jit(solution)/shard_map/pair_rows/pallas_call | solution.py:390
  30.0 1.6 %collective-permute-start.6 = (f32[192,384]{1,0:T(8,128)S(1)}, f32[192,384]{1,0:T(8,128)S(1)}, u32[]{:S(2)}, u32[]{:S(2)}) collective-permute-start(f32[192,384]{1,0:T(8,128)S(1)} %get-tuple-element.96.three_ref), channel_id=1, source_target_pairs={{0,16},{8,24},{16,0},{24,8},{1,17},{9,25},{17,1},{25,9},{2,18},{10... | collective-permute-start | bytes 884744 | tf_op jit(solution)/shard_map/ppermute | solution.py:21
  31.6 3.5 %far_level.1 = (f32[384,192]{1,0:T(8,128)S(1)}, f32[384,384]{1,0:T(8,128)S(1)}) custom-call(f32[200,384]{1,0:T(8,128)S(1)} %collective-permute-done.1.own_ref, f32[200,384]{1,0:T(8,128)S(1)} %collective-permute-done.3.sib_ref, f32[384,384]{1,0:T(8,128)S(1)} %copy-done.2), custom_call_target="tpu_custom_call" | custom-call | flops 1800000000 | tf_op jit(solution)/shard_map/far_level/pallas_call | solution.py:390
  35.1 4.9 %face_start.1 = (f32[384,384]{1,0:T(8,128)S(1)}, f32[8,128]{1,0:T(8,128)S(1)}) custom-call(f32[200,384]{1,0:T(8,128)S(1)} %pack.1.own_ref.one_ref, f32[384,384]{1,0:T(8,128)S(1)} %get-tuple-element.78.sum_ref), custom_call_target="tpu_custom_call" | custom-call | flops 1800000000 | tf_op jit(solution)/shard_map/face_start/pallas_call | solution.py:390
  40.6 1.6 %collective-permute-start.7 = (f32[192,128]{1,0:T(8,128)S(1)}, f32[192,128]{1,0:T(8,128)S(1)}, u32[]{:S(2)}, u32[]{:S(2)}) collective-permute-start(f32[192,128]{1,0:T(8,128)S(1)} %get-tuple-element.100), channel_id=1, source_target_pairs={{0,4},{1,5},{2,6},{3,7},{4,0},{5,1},{6,2},{7,3},{8,12},{9,13},{10,... | collective-permute-start | bytes 294920 | tf_op jit(solution)/shard_map/ppermute | solution.py:21
  42.2 1.4 %collective-permute-start.8 = (f32[128,384]{1,0:T(8,128)S(1)}, f32[128,384]{1,0:T(8,128)S(1)}, u32[]{:S(2)}, u32[]{:S(2)}) collective-permute-start(f32[128,384]{1,0:T(8,128)S(1)} %get-tuple-element.106), channel_id=1, source_target_pairs={{0,4},{1,5},{2,6},{3,7},{4,0},{5,1},{6,2},{7,3},{8,12},{9,13},{10,... | collective-permute-start | bytes 589832 | tf_op jit(solution)/shard_map/ppermute | solution.py:21
  43.6 1.5 %collective-permute-start.10 = (f32[128,384]{1,0:T(8,128)S(1)}, f32[128,384]{1,0:T(8,128)S(1)}, u32[]{:S(2)}, u32[]{:S(2)}) collective-permute-start(f32[128,384]{1,0:T(8,128)S(1)} %collective-permute-done.4.three_c), channel_id=1, source_target_pairs={{0,16},{8,24},{16,0},{24,8},{1,17},{9,25},{17,1},{25,9},{2,18},{10... | collective-permute-start | bytes 589832 | tf_op jit(solution)/shard_map/ppermute | solution.py:21
  45.1 2.9 %face_end.1.inv2_ref = f32[384,384]{1,0:T(8,128)S(1)} custom-call(f32[384,384]{1,0:T(8,128)S(1)} %get-tuple-element.78.sum_ref, f32[384,384]{1,0:T(8,128)S(1)} %get-tuple-element.90.start_ref, f32[8,128]{1,0:T(8,128)S(1)} %get-tuple-element.91.bound_ref), custom_call_target="tpu_custom_call" | custom-call | flops 1200000000 | tf_op jit(solution)/shard_map/face_end/pallas_call | solution.py:390
  48.0 2.3 %near_rows.1 = (f32[384,384]{1,0:T(8,128)S(1)}, f32[384,384]{1,0:T(8,128)S(1)}, f32[384,384]{1,0:T(8,128)S(1)}, f32[384,384]{1,0:T(8,128)S(1)}) custom-call(f32[384,384]{1,0:T(8,128)S(1)} %face_end.1.inv2_ref, f32[384,384]{1,0:T(8,128)S(1)} %get-tuple-element.92.rows_a, f32[384,384]{1,0:T(8,128)S(1)} %get-tuple-element.93.rows_b, ...), custom_call_target="tpu_custom_call" | custom-call | flops 1000000000 | tf_op jit(solution)/shard_map/near_rows/pallas_call | solution.py:390
  50.3 2.1 %collective-permute-done.7 = f32[192,128]{1,0:T(8,128)S(1)} collective-permute-done((f32[192,128]{1,0:T(8,128)S(1)}, f32[192,128]{1,0:T(8,128)S(1)}, u32[]{:S(2)}, u32[]{:S(2)}) %collective-permute-start.7) | collective-permute-done | bytes 98336 | tf_op jit(solution)/shard_map/ppermute | solution.py:21
  52.4 1.6 %collective-permute-start.12 = (f32[192,128]{1,0:T(8,128)S(1)}, f32[192,128]{1,0:T(8,128)S(1)}, u32[]{:S(2)}, u32[]{:S(2)}) collective-permute-start(f32[192,128]{1,0:T(8,128)S(1)} %add.17.total_ref), channel_id=1, source_target_pairs={{0,16},{8,24},{16,0},{24,8},{1,17},{9,25},{17,1},{25,9},{2,18},{10... | collective-permute-start | bytes 294920 | tf_op jit(solution)/shard_map/ppermute | solution.py:21
  54.5 1.5 %collective-permute-start.11 = (f32[128,384]{1,0:T(8,128)S(1)}, f32[128,384]{1,0:T(8,128)S(1)}, u32[]{:S(2)}, u32[]{:S(2)}) collective-permute-start(f32[128,384]{1,0:T(8,128)S(1)} %collective-permute-done.8.four_c), channel_id=1, source_target_pairs={{0,16},{8,24},{16,0},{24,8},{1,17},{9,25},{17,1},{25,9},{2,18},{10... | collective-permute-start | bytes 589832 | tf_op jit(solution)/shard_map/ppermute | solution.py:21
  56.0 2.8 %cross_rows.1 = (f32[384,1536]{1,0:T(8,128)}, f32[384,384]{1,0:T(8,128)S(1)}, f32[384,192]{1,0:T(8,128)S(1)}, f32[384,128]{1,0:T(8,128)S(1)}) custom-call(s32[4]{0:T(128)S(1)} %pad_add_fusion.place_ref, f32[384,192]{1,0:T(8,128)} %get-tuple-element.71.fold_any, f32[192,128]{1,0:T(8,128)} %get-tuple-element.72.shift_any, ...), custom_call_target="tpu_custom_call" | custom-call | flops 1000000000 | tf_op jit(solution)/shard_map/cross_rows/pallas_call | solution.py:390
  58.8 1.3 %collective-permute-done.11.four_d = f32[128,384]{1,0:T(8,128)S(1)} collective-permute-done((f32[128,384]{1,0:T(8,128)S(1)}, f32[128,384]{1,0:T(8,128)S(1)}, u32[]{:S(2)}, u32[]{:S(2)}) %collective-permute-start.11) | collective-permute-done | bytes 196640 | tf_op jit(solution)/shard_map/ppermute | solution.py:21
  60.2 1.9 %last_rows.1 = (f32[384,1536]{1,0:T(8,128)}, f32[384,128]{1,0:T(8,128)}) custom-call(s32[4]{0:T(128)S(1)} %pad_add_fusion.place_ref, f32[384,1536]{1,0:T(8,128)} %get-tuple-element.110.in_any, f32[384,384]{1,0:T(8,128)S(1)} %get-tuple-element.111.part_d, f32[384,384]{1,0:T(8,128)S(1)} %get-tuple-element.103.left_d, ...), custom_call_target="tpu_custom_call", output_to_operand_aliasing={{0}: (1, {})} | custom-call | flops 1000000000 | tf_op jit(solution)/shard_map/last_rows/pallas_call | solution.py:390
  (21 shorter events, 3.8 us)
Async XLA Ops:
  2.0 10.3 %collective-permute-start = (f32[200,384]{1,0:T(8,128)S(1)}, f32[200,384]{1,0:T(8,128)S(1)}, u32[]{:S(2)}, u32[]{:S(2)}) collective-permute-start(f32[200,384]{1,0:T(8,128)S(1)} %pack.1.own_ref.one_ref), channel_id=1, source_target_pairs={{0,16},{8,24},{16,0},{24,8},{1,17},{9,25},{17,1},{25,9},{2,18},{10... | collective-permute-start | bytes 921608 | tf_op jit(solution)/shard_map/ppermute | solution.py:21
  5.0 16.2 %collective-permute-start.1 = (f32[200,384]{1,0:T(8,128)S(1)}, f32[200,384]{1,0:T(8,128)S(1)}, u32[]{:S(2)}, u32[]{:S(2)}) collective-permute-start(f32[200,384]{1,0:T(8,128)S(1)} %pack.1.own_ref.one_ref), channel_id=1, source_target_pairs={{0,4},{1,5},{2,6},{3,7},{4,0},{5,1},{6,2},{7,3},{8,12},{9,13},{10,... | collective-permute-start | bytes 921608 | tf_op jit(solution)/shard_map/ppermute | solution.py:21
  12.2 10.3 %copy-start = (f32[1,1,384,128]{3,2,1,0:T(8,128)S(1)}, f32[1,1,384,128]{3,2,1,0:T(8,128)}, u32[]{:S(2)}) copy-start(f32[1,1,384,128]{3,2,1,0:T(8,128)} %param.7) | copy-start | bytes 589828
  12.2 10.3 %collective-permute-start.2 = (f32[256,384]{1,0:T(8,128)S(1)}, f32[256,384]{1,0:T(8,128)S(1)}, u32[]{:S(2)}, u32[]{:S(2)}) collective-permute-start(f32[256,384]{1,0:T(8,128)S(1)} %get-tuple-element.66.more_a), channel_id=1, source_target_pairs={{0,16},{8,24},{16,0},{24,8},{1,17},{9,25},{17,1},{25,9},{2,18},{10... | collective-permute-start | bytes 1179656 | tf_op jit(solution)/shard_map/ppermute | solution.py:21
  17.6 0.8 %copy-start.1 = (f32[384,384]{1,0:T(8,128)}, f32[384,384]{1,0:T(8,128)S(1)}, u32[]{:S(2)}) copy-start(f32[384,384]{1,0:T(8,128)S(1)} %get-tuple-element.77.near_ref) | copy-start | bytes 1769476
  21.2 8.8 %collective-permute-start.3 = (f32[200,384]{1,0:T(8,128)S(1)}, f32[200,384]{1,0:T(8,128)S(1)}, u32[]{:S(2)}, u32[]{:S(2)}) collective-permute-start(f32[200,384]{1,0:T(8,128)S(1)} %collective-permute-done.1.own_ref), channel_id=1, source_target_pairs={{0,16},{8,24},{16,0},{24,8},{1,17},{9,25},{17,1},{25,9},{2,18},{10... | collective-permute-start | bytes 921608 | tf_op jit(solution)/shard_map/ppermute | solution.py:21
  21.7 18.4 %collective-permute-start.5 = (f32[128,384]{1,0:T(8,128)S(1)}, f32[128,384]{1,0:T(8,128)S(1)}, u32[]{:S(2)}, u32[]{:S(2)}) collective-permute-start(f32[128,384]{1,0:T(8,128)S(1)} %get-tuple-element.82), channel_id=1, source_target_pairs={{0,4},{1,5},{2,6},{3,7},{4,0},{5,1},{6,2},{7,3},{8,12},{9,13},{10,... | collective-permute-start | bytes 589832 | tf_op jit(solution)/shard_map/ppermute | solution.py:21
  22.9 8.7 %copy-start.2 = (f32[384,384]{1,0:T(8,128)S(1)}, f32[384,384]{1,0:T(8,128)}, u32[]{:S(2)}) copy-start(f32[384,384]{1,0:T(8,128)} %copy-done.1) | copy-start | bytes 1769476
  22.9 20.6 %collective-permute-start.4 = (f32[128,384]{1,0:T(8,128)S(1)}, f32[128,384]{1,0:T(8,128)S(1)}, u32[]{:S(2)}, u32[]{:S(2)}) collective-permute-start(f32[128,384]{1,0:T(8,128)S(1)} %get-tuple-element.79), channel_id=1, source_target_pairs={{0,4},{1,5},{2,6},{3,7},{4,0},{5,1},{6,2},{7,3},{8,12},{9,13},{10,... | collective-permute-start | bytes 589832 | tf_op jit(solution)/shard_map/ppermute | solution.py:21
  30.0 17.9 %collective-permute-start.6 = (f32[192,384]{1,0:T(8,128)S(1)}, f32[192,384]{1,0:T(8,128)S(1)}, u32[]{:S(2)}, u32[]{:S(2)}) collective-permute-start(f32[192,384]{1,0:T(8,128)S(1)} %get-tuple-element.96.three_ref), channel_id=1, source_target_pairs={{0,16},{8,24},{16,0},{24,8},{1,17},{9,25},{17,1},{25,9},{2,18},{10... | collective-permute-start | bytes 884744 | tf_op jit(solution)/shard_map/ppermute | solution.py:21
  40.0 16.0 %collective-permute-start.9 = (f32[128,384]{1,0:T(8,128)S(1)}, f32[128,384]{1,0:T(8,128)S(1)}, u32[]{:S(2)}, u32[]{:S(2)}) collective-permute-start(f32[128,384]{1,0:T(8,128)S(1)} %collective-permute-done.5.two_c), channel_id=1, source_target_pairs={{0,16},{8,24},{16,0},{24,8},{1,17},{9,25},{17,1},{25,9},{2,18},{10... | collective-permute-start | bytes 589832 | tf_op jit(solution)/shard_map/ppermute | solution.py:21
  40.6 11.7 %collective-permute-start.7 = (f32[192,128]{1,0:T(8,128)S(1)}, f32[192,128]{1,0:T(8,128)S(1)}, u32[]{:S(2)}, u32[]{:S(2)}) collective-permute-start(f32[192,128]{1,0:T(8,128)S(1)} %get-tuple-element.100), channel_id=1, source_target_pairs={{0,4},{1,5},{2,6},{3,7},{4,0},{5,1},{6,2},{7,3},{8,12},{9,13},{10,... | collective-permute-start | bytes 294920 | tf_op jit(solution)/shard_map/ppermute | solution.py:21
  42.2 12.3 %collective-permute-start.8 = (f32[128,384]{1,0:T(8,128)S(1)}, f32[128,384]{1,0:T(8,128)S(1)}, u32[]{:S(2)}, u32[]{:S(2)}) collective-permute-start(f32[128,384]{1,0:T(8,128)S(1)} %get-tuple-element.106), channel_id=1, source_target_pairs={{0,4},{1,5},{2,6},{3,7},{4,0},{5,1},{6,2},{7,3},{8,12},{9,13},{10,... | collective-permute-start | bytes 589832 | tf_op jit(solution)/shard_map/ppermute | solution.py:21
  43.6 12.5 %collective-permute-start.10 = (f32[128,384]{1,0:T(8,128)S(1)}, f32[128,384]{1,0:T(8,128)S(1)}, u32[]{:S(2)}, u32[]{:S(2)}) collective-permute-start(f32[128,384]{1,0:T(8,128)S(1)} %collective-permute-done.4.three_c), channel_id=1, source_target_pairs={{0,16},{8,24},{16,0},{24,8},{1,17},{9,25},{17,1},{25,9},{2,18},{10... | collective-permute-start | bytes 589832 | tf_op jit(solution)/shard_map/ppermute | solution.py:21
  52.4 6.4 %collective-permute-start.12 = (f32[192,128]{1,0:T(8,128)S(1)}, f32[192,128]{1,0:T(8,128)S(1)}, u32[]{:S(2)}, u32[]{:S(2)}) collective-permute-start(f32[192,128]{1,0:T(8,128)S(1)} %add.17.total_ref), channel_id=1, source_target_pairs={{0,16},{8,24},{16,0},{24,8},{1,17},{9,25},{17,1},{25,9},{2,18},{10... | collective-permute-start | bytes 294920 | tf_op jit(solution)/shard_map/ppermute | solution.py:21
  54.5 5.7 %collective-permute-start.11 = (f32[128,384]{1,0:T(8,128)S(1)}, f32[128,384]{1,0:T(8,128)S(1)}, u32[]{:S(2)}, u32[]{:S(2)}) collective-permute-start(f32[128,384]{1,0:T(8,128)S(1)} %collective-permute-done.8.four_c), channel_id=1, source_target_pairs={{0,16},{8,24},{16,0},{24,8},{1,17},{9,25},{17,1},{25,9},{2,18},{10... | collective-permute-start | bytes 589832 | tf_op jit(solution)/shard_map/ppermute | solution.py:21

commit v4 on v3

--- a/solution.py
+++ b/solution.py
@@ -64,7 +64,7 @@
     return (rows_of((n, n)) == cols_of((n, n))).astype(f32)
 
 
-def invert_start(mat, least, inv_ref, res_ref):
+def invert_start(mat, least, inv_ref, res_ref, enough=0.02):
     n = mat.shape[0]
     unit = eye(n)
     most = jnp.max(jnp.sum(jnp.abs(mat), axis=0, keepdims=True))
@@ -99,7 +99,7 @@
         return gain * eps * eps * 0.5, 2.0 * gain * eps * noise + 3e-5
 
     eps, noise = lax.while_loop(
-        lambda carry: carry[0] > 0.02, fast, (gain * eps * eps * 0.5, jnp.float32(6e-5))
+        lambda carry: carry[0] > enough, fast, (gain * eps * eps * 0.5, jnp.float32(6e-5))
     )
     return jnp.minimum(eps + noise + 1e-5 * (most / least), 0.5)
 
@@ -244,7 +244,7 @@
 
 
 def face_start_kernel(own_ref, sum_ref, inv_ref, bound_ref, res):
-    bound = invert_start(sum_ref[...], least_of(own_ref), inv_ref, res)
+    bound = invert_start(sum_ref[...], least_of(own_ref), inv_ref, res, 0.1)
     bound_ref[...] = jnp.zeros(bound_ref.shape, f32) + bound
 
 

time: 62.4 us -> 61.4 us (0.984)
  waiting for transfers between devices: 10.8 us -> 8.75 us
  Pallas kernels: 27.4 us -> 28.7 us
    ppermute x13, waiting for transfers between devices: 10.8 us -> 8.75 us  [shifted(): lax.ppermute(shard, axis, [(i, (i + size // 2) % size) for i in range(siz...]
    pallas_call x11, Pallas kernels: 27.4 us -> 28.7 us  [call(): pl.pallas_call(kernel, out_shape=[pltpu.HBM(s, f32) if spec is HBM else j...]
  transfers between devices with their start and end apart: 13 -> 13, of which waited for: 6 -> 5; matrix products, arithmetic and copies ran while one was open for 0% -> 0% of each run, Pallas kernels for 39% -> 42%
where the time goes in v4:
time: 61.4 us; the launch traced here: 61.2 us
  Pallas kernels  28.7 us (47%)
  starting transfers between devices  21.9 us (36%)
  waiting for transfers between devices  8.75 us (14%)
  between operations  0.94 us (2%)
  local copies, waits for them, and re-layouts  0.82 us (1%)
    pallas_call x11, Pallas kernels, call(): pl.pallas_call(kernel, out_shape=[pltpu.HBM(s, f32) if spec is HBM else j...  28.7 us
    ppermute x13, starting transfers between devices, shifted(): lax.ppermute(shard, axis, [(i, (i + size // 2) % size) for i in range(siz...  21.9 us
    ppermute x13, waiting for transfers between devices, shifted(): lax.ppermute(shard, axis, [(i, (i + size // 2) % size) for i in range(siz...  8.75 us
  transfers between devices with their start and end apart: 13, of which 5 were waited for; matrix products, arithmetic and copies ran while one was open for 0% of the time, Pallas kernels for 42%

profile of v4, /device:TPU:0, one launch (start us, length us, event | category | flops | bytes accessed | tf_op | source)
XLA Modules:
  0.0 61.2 jit_solution(8531438891404311339)
XLA Ops:
  0.6 1.3 %pack.1.own_ref.one_ref = f32[200,384]{1,0:T(8,128)S(1)} custom-call(s32[12]{0:T(128)} %bitcast.16, f32[8]{0:T(128)} %table_any.1, f32[768,768]{1,0:T(8,128)} %bitcast.11), custom_call_target="tpu_custom_call" | custom-call | flops 1000000000 | tf_op jit(solution)/shard_map/pack/pallas_call | solution.py:390
  2.0 3.0 %collective-permute-start = (f32[200,384]{1,0:T(8,128)S(1)}, f32[200,384]{1,0:T(8,128)S(1)}, u32[]{:S(2)}, u32[]{:S(2)}) collective-permute-start(f32[200,384]{1,0:T(8,128)S(1)} %pack.1.own_ref.one_ref), channel_id=1, source_target_pairs={{0,16},{8,24},{16,0},{24,8},{1,17},{9,25},{17,1},{25,9},{2,18},{10... | collective-permute-start | bytes 921608 | tf_op jit(solution)/shard_map/ppermute | solution.py:21
  5.0 2.6 %collective-permute-start.1 = (f32[200,384]{1,0:T(8,128)S(1)}, f32[200,384]{1,0:T(8,128)S(1)}, u32[]{:S(2)}, u32[]{:S(2)}) collective-permute-start(f32[200,384]{1,0:T(8,128)S(1)} %pack.1.own_ref.one_ref), channel_id=1, source_target_pairs={{0,4},{1,5},{2,6},{3,7},{4,0},{5,1},{6,2},{7,3},{8,12},{9,13},{10,... | collective-permute-start | bytes 921608 | tf_op jit(solution)/shard_map/ppermute | solution.py:21
  7.6 1.5 %outer.1 = (f32[128,384]{1,0:T(8,128)S(1)}, f32[128,384]{1,0:T(8,128)S(1)}, f32[128,384]{1,0:T(8,128)S(1)}, f32[192,384]{1,0:T(8,128)S(1)}, f32[256,384]{1,0:T(8,128)S(1)}) custom-call(f32[768,768]{1,0:T(8,128)} %bitcast.12, f32[384,128]{1,0:T(8,128)} %bitcast.9), custom_call_target="tpu_custom_call" | custom-call | flops 1000000000 | tf_op jit(solution)/shard_map/outer/pallas_call | solution.py:390
  9.0 3.2 %collective-permute-done.sib_ref = f32[200,384]{1,0:T(8,128)S(1)} collective-permute-done((f32[200,384]{1,0:T(8,128)S(1)}, f32[200,384]{1,0:T(8,128)S(1)}, u32[]{:S(2)}, u32[]{:S(2)}) %collective-permute-start) | collective-permute-done | bytes 307232 | tf_op jit(solution)/shard_map/ppermute | solution.py:21
  12.2 1.7 %collective-permute-start.2 = (f32[256,384]{1,0:T(8,128)S(1)}, f32[256,384]{1,0:T(8,128)S(1)}, u32[]{:S(2)}, u32[]{:S(2)}) collective-permute-start(f32[256,384]{1,0:T(8,128)S(1)} %get-tuple-element.66.more_a), channel_id=1, source_target_pairs={{0,16},{8,24},{16,0},{24,8},{1,17},{9,25},{17,1},{25,9},{2,18},{10... | collective-permute-start | bytes 1179656 | tf_op jit(solution)/shard_map/ppermute | solution.py:21
  14.0 3.6 %own_level.1 = (f32[192,192]{1,0:T(8,128)S(1)}, f32[384,192]{1,0:T(8,128)S(1)}, f32[384,384]{1,0:T(8,128)S(1)}) custom-call(f32[200,384]{1,0:T(8,128)S(1)} %pack.1.own_ref.one_ref, f32[200,384]{1,0:T(8,128)S(1)} %collective-permute-done.sib_ref), custom_call_target="tpu_custom_call" | custom-call | flops 1500000000 | tf_op jit(solution)/shard_map/own_level/pallas_call | solution.py:390
  18.4 2.8 %collective-permute-done.1.own_ref = f32[200,384]{1,0:T(8,128)S(1)} collective-permute-done((f32[200,384]{1,0:T(8,128)S(1)}, f32[200,384]{1,0:T(8,128)S(1)}, u32[]{:S(2)}, u32[]{:S(2)}) %collective-permute-start.1) | collective-permute-done | bytes 307232 | tf_op jit(solution)/shard_map/ppermute | solution.py:21
  22.9 4.7 %collective-permute-start.4 = (f32[128,384]{1,0:T(8,128)S(1)}, f32[128,384]{1,0:T(8,128)S(1)}, u32[]{:S(2)}, u32[]{:S(2)}) collective-permute-start(f32[128,384]{1,0:T(8,128)S(1)} %get-tuple-element.79), channel_id=1, source_target_pairs={{0,4},{1,5},{2,6},{3,7},{4,0},{5,1},{6,2},{7,3},{8,12},{9,13},{10,... | collective-permute-start | bytes 589832 | tf_op jit(solution)/shard_map/ppermute | solution.py:21
  27.6 2.4 %pair_rows.1 = (f32[384,384]{1,0:T(8,128)S(1)}, f32[384,384]{1,0:T(8,128)S(1)}, f32[384,384]{1,0:T(8,128)S(1)}, f32[384,384]{1,0:T(8,128)S(1)}, f32[384,192]{1,0:T(8,128)}, /*index=5*/f32[192,128]{1,0:T(8,128)}) custom-call(f32[768,768]{1,0:T(8,128)} %bitcast.13, f32[200,384]{1,0:T(8,128)S(1)} %pack.1.own_ref.one_ref, ...), custom_call_target="tpu_custom_call" | custom-call | flops 1000000000 | tf_op jit(solution)/shard_map/pair_rows/pallas_call | solution.py:390
  30.0 1.6 %collective-permute-start.6 = (f32[192,384]{1,0:T(8,128)S(1)}, f32[192,384]{1,0:T(8,128)S(1)}, u32[]{:S(2)}, u32[]{:S(2)}) collective-permute-start(f32[192,384]{1,0:T(8,128)S(1)} %get-tuple-element.96.three_ref), channel_id=1, source_target_pairs={{0,16},{8,24},{16,0},{24,8},{1,17},{9,25},{17,1},{25,9},{2,18},{10... | collective-permute-start | bytes 884744 | tf_op jit(solution)/shard_map/ppermute | solution.py:21
  31.6 3.5 %far_level.1 = (f32[384,192]{1,0:T(8,128)S(1)}, f32[384,384]{1,0:T(8,128)S(1)}) custom-call(f32[200,384]{1,0:T(8,128)S(1)} %collective-permute-done.1.own_ref, f32[200,384]{1,0:T(8,128)S(1)} %collective-permute-done.3.sib_ref, f32[384,384]{1,0:T(8,128)S(1)} %copy-done.2), custom_call_target="tpu_custom_call" | custom-call | flops 1800000000 | tf_op jit(solution)/shard_map/far_level/pallas_call | solution.py:390
  35.1 3.9 %face_start.1 = (f32[384,384]{1,0:T(8,128)S(1)}, f32[8,128]{1,0:T(8,128)S(1)}) custom-call(f32[200,384]{1,0:T(8,128)S(1)} %pack.1.own_ref.one_ref, f32[384,384]{1,0:T(8,128)S(1)} %get-tuple-element.78.sum_ref), custom_call_target="tpu_custom_call" | custom-call | flops 1800000000 | tf_op jit(solution)/shard_map/face_start/pallas_call | solution.py:390
  39.1 1.0 %collective-permute-start.9 = (f32[128,384]{1,0:T(8,128)S(1)}, f32[128,384]{1,0:T(8,128)S(1)}, u32[]{:S(2)}, u32[]{:S(2)}) collective-permute-start(f32[128,384]{1,0:T(8,128)S(1)} %collective-permute-done.5.two_c), channel_id=1, source_target_pairs={{0,16},{8,24},{16,0},{24,8},{1,17},{9,25},{17,1},{25,9},{2,18},{10... | collective-permute-start | bytes 589832 | tf_op jit(solution)/shard_map/ppermute | solution.py:21
  40.1 1.1 %collective-permute-start.7 = (f32[192,128]{1,0:T(8,128)S(1)}, f32[192,128]{1,0:T(8,128)S(1)}, u32[]{:S(2)}, u32[]{:S(2)}) collective-permute-start(f32[192,128]{1,0:T(8,128)S(1)} %get-tuple-element.100), channel_id=1, source_target_pairs={{0,4},{1,5},{2,6},{3,7},{4,0},{5,1},{6,2},{7,3},{8,12},{9,13},{10,... | collective-permute-start | bytes 294920 | tf_op jit(solution)/shard_map/ppermute | solution.py:21
  41.2 1.8 %collective-permute-start.8 = (f32[128,384]{1,0:T(8,128)S(1)}, f32[128,384]{1,0:T(8,128)S(1)}, u32[]{:S(2)}, u32[]{:S(2)}) collective-permute-start(f32[128,384]{1,0:T(8,128)S(1)} %get-tuple-element.106), channel_id=1, source_target_pairs={{0,4},{1,5},{2,6},{3,7},{4,0},{5,1},{6,2},{7,3},{8,12},{9,13},{10,... | collective-permute-start | bytes 589832 | tf_op jit(solution)/shard_map/ppermute | solution.py:21
  43.0 1.1 %collective-permute-start.10 = (f32[128,384]{1,0:T(8,128)S(1)}, f32[128,384]{1,0:T(8,128)S(1)}, u32[]{:S(2)}, u32[]{:S(2)}) collective-permute-start(f32[128,384]{1,0:T(8,128)S(1)} %collective-permute-done.4.three_c), channel_id=1, source_target_pairs={{0,16},{8,24},{16,0},{24,8},{1,17},{9,25},{17,1},{25,9},{2,18},{10... | collective-permute-start | bytes 589832 | tf_op jit(solution)/shard_map/ppermute | solution.py:21
  44.1 5.1 %face_end.1.inv2_ref = f32[384,384]{1,0:T(8,128)S(1)} custom-call(f32[384,384]{1,0:T(8,128)S(1)} %get-tuple-element.78.sum_ref, f32[384,384]{1,0:T(8,128)S(1)} %get-tuple-element.90.start_ref, f32[8,128]{1,0:T(8,128)S(1)} %get-tuple-element.91.bound_ref), custom_call_target="tpu_custom_call" | custom-call | flops 1200000000 | tf_op jit(solution)/shard_map/face_end/pallas_call | solution.py:390
  49.2 2.3 %near_rows.1 = (f32[384,384]{1,0:T(8,128)S(1)}, f32[384,384]{1,0:T(8,128)S(1)}, f32[384,384]{1,0:T(8,128)S(1)}, f32[384,384]{1,0:T(8,128)S(1)}) custom-call(f32[384,384]{1,0:T(8,128)S(1)} %face_end.1.inv2_ref, f32[384,384]{1,0:T(8,128)S(1)} %get-tuple-element.92.rows_a, f32[384,384]{1,0:T(8,128)S(1)} %get-tuple-element.93.rows_b, ...), custom_call_target="tpu_custom_call" | custom-call | flops 1000000000 | tf_op jit(solution)/shard_map/near_rows/pallas_call | solution.py:390
  51.6 1.4 %collective-permute-start.12 = (f32[192,128]{1,0:T(8,128)S(1)}, f32[192,128]{1,0:T(8,128)S(1)}, u32[]{:S(2)}, u32[]{:S(2)}) collective-permute-start(f32[192,128]{1,0:T(8,128)S(1)} %add.17.total_ref), channel_id=1, source_target_pairs={{0,16},{8,24},{16,0},{24,8},{1,17},{9,25},{17,1},{25,9},{2,18},{10... | collective-permute-start | bytes 294920 | tf_op jit(solution)/shard_map/ppermute | solution.py:21
  53.5 1.5 %collective-permute-start.11 = (f32[128,384]{1,0:T(8,128)S(1)}, f32[128,384]{1,0:T(8,128)S(1)}, u32[]{:S(2)}, u32[]{:S(2)}) collective-permute-start(f32[128,384]{1,0:T(8,128)S(1)} %collective-permute-done.8.four_c), channel_id=1, source_target_pairs={{0,16},{8,24},{16,0},{24,8},{1,17},{9,25},{17,1},{25,9},{2,18},{10... | collective-permute-start | bytes 589832 | tf_op jit(solution)/shard_map/ppermute | solution.py:21
  55.1 2.8 %cross_rows.1 = (f32[384,1536]{1,0:T(8,128)}, f32[384,384]{1,0:T(8,128)S(1)}, f32[384,192]{1,0:T(8,128)S(1)}, f32[384,128]{1,0:T(8,128)S(1)}) custom-call(s32[4]{0:T(128)S(1)} %pad_add_fusion.place_ref, f32[384,192]{1,0:T(8,128)} %get-tuple-element.71.fold_any, f32[192,128]{1,0:T(8,128)} %get-tuple-element.72.shift_any, ...), custom_call_target="tpu_custom_call" | custom-call | flops 1000000000 | tf_op jit(solution)/shard_map/cross_rows/pallas_call | solution.py:390
  57.9 1.3 %collective-permute-done.11.four_d = f32[128,384]{1,0:T(8,128)S(1)} collective-permute-done((f32[128,384]{1,0:T(8,128)S(1)}, f32[128,384]{1,0:T(8,128)S(1)}, u32[]{:S(2)}, u32[]{:S(2)}) %collective-permute-start.11) | collective-permute-done | bytes 196640 | tf_op jit(solution)/shard_map/ppermute | solution.py:21
  59.2 1.9 %last_rows.1 = (f32[384,1536]{1,0:T(8,128)}, f32[384,128]{1,0:T(8,128)}) custom-call(s32[4]{0:T(128)S(1)} %pad_add_fusion.place_ref, f32[384,1536]{1,0:T(8,128)} %get-tuple-element.110.in_any, f32[384,384]{1,0:T(8,128)S(1)} %get-tuple-element.111.part_d, f32[384,384]{1,0:T(8,128)S(1)} %get-tuple-element.103.left_d, ...), custom_call_target="tpu_custom_call", output_to_operand_aliasing={{0}: (1, {})} | custom-call | flops 1000000000 | tf_op jit(solution)/shard_map/last_rows/pallas_call | solution.py:390
  (21 shorter events, 3.2 us)
Async XLA Ops:
  2.0 10.3 %collective-permute-start = (f32[200,384]{1,0:T(8,128)S(1)}, f32[200,384]{1,0:T(8,128)S(1)}, u32[]{:S(2)}, u32[]{:S(2)}) collective-permute-start(f32[200,384]{1,0:T(8,128)S(1)} %pack.1.own_ref.one_ref), channel_id=1, source_target_pairs={{0,16},{8,24},{16,0},{24,8},{1,17},{9,25},{17,1},{25,9},{2,18},{10... | collective-permute-start | bytes 921608 | tf_op jit(solution)/shard_map/ppermute | solution.py:21
  5.0 16.2 %collective-permute-start.1 = (f32[200,384]{1,0:T(8,128)S(1)}, f32[200,384]{1,0:T(8,128)S(1)}, u32[]{:S(2)}, u32[]{:S(2)}) collective-permute-start(f32[200,384]{1,0:T(8,128)S(1)} %pack.1.own_ref.one_ref), channel_id=1, source_target_pairs={{0,4},{1,5},{2,6},{3,7},{4,0},{5,1},{6,2},{7,3},{8,12},{9,13},{10,... | collective-permute-start | bytes 921608 | tf_op jit(solution)/shard_map/ppermute | solution.py:21
  12.2 10.3 %copy-start = (f32[1,1,384,128]{3,2,1,0:T(8,128)S(1)}, f32[1,1,384,128]{3,2,1,0:T(8,128)}, u32[]{:S(2)}) copy-start(f32[1,1,384,128]{3,2,1,0:T(8,128)} %param.7) | copy-start | bytes 589828
  12.2 10.3 %collective-permute-start.2 = (f32[256,384]{1,0:T(8,128)S(1)}, f32[256,384]{1,0:T(8,128)S(1)}, u32[]{:S(2)}, u32[]{:S(2)}) collective-permute-start(f32[256,384]{1,0:T(8,128)S(1)} %get-tuple-element.66.more_a), channel_id=1, source_target_pairs={{0,16},{8,24},{16,0},{24,8},{1,17},{9,25},{17,1},{25,9},{2,18},{10... | collective-permute-start | bytes 1179656 | tf_op jit(solution)/shard_map/ppermute | solution.py:21
  17.6 0.8 %copy-start.1 = (f32[384,384]{1,0:T(8,128)}, f32[384,384]{1,0:T(8,128)S(1)}, u32[]{:S(2)}) copy-start(f32[384,384]{1,0:T(8,128)S(1)} %get-tuple-element.77.near_ref) | copy-start | bytes 1769476
  21.2 8.8 %collective-permute-start.3 = (f32[200,384]{1,0:T(8,128)S(1)}, f32[200,384]{1,0:T(8,128)S(1)}, u32[]{:S(2)}, u32[]{:S(2)}) collective-permute-start(f32[200,384]{1,0:T(8,128)S(1)} %collective-permute-done.1.own_ref), channel_id=1, source_target_pairs={{0,16},{8,24},{16,0},{24,8},{1,17},{9,25},{17,1},{25,9},{2,18},{10... | collective-permute-start | bytes 921608 | tf_op jit(solution)/shard_map/ppermute | solution.py:21
  21.7 17.4 %collective-permute-start.5 = (f32[128,384]{1,0:T(8,128)S(1)}, f32[128,384]{1,0:T(8,128)S(1)}, u32[]{:S(2)}, u32[]{:S(2)}) collective-permute-start(f32[128,384]{1,0:T(8,128)S(1)} %get-tuple-element.82), channel_id=1, source_target_pairs={{0,4},{1,5},{2,6},{3,7},{4,0},{5,1},{6,2},{7,3},{8,12},{9,13},{10,... | collective-permute-start | bytes 589832 | tf_op jit(solution)/shard_map/ppermute | solution.py:21
  22.9 8.7 %copy-start.2 = (f32[384,384]{1,0:T(8,128)S(1)}, f32[384,384]{1,0:T(8,128)}, u32[]{:S(2)}) copy-start(f32[384,384]{1,0:T(8,128)} %copy-done.1) | copy-start | bytes 1769476
  22.9 20.1 %collective-permute-start.4 = (f32[128,384]{1,0:T(8,128)S(1)}, f32[128,384]{1,0:T(8,128)S(1)}, u32[]{:S(2)}, u32[]{:S(2)}) collective-permute-start(f32[128,384]{1,0:T(8,128)S(1)} %get-tuple-element.79), channel_id=1, source_target_pairs={{0,4},{1,5},{2,6},{3,7},{4,0},{5,1},{6,2},{7,3},{8,12},{9,13},{10,... | collective-permute-start | bytes 589832 | tf_op jit(solution)/shard_map/ppermute | solution.py:21
  30.0 19.2 %collective-permute-start.6 = (f32[192,384]{1,0:T(8,128)S(1)}, f32[192,384]{1,0:T(8,128)S(1)}, u32[]{:S(2)}, u32[]{:S(2)}) collective-permute-start(f32[192,384]{1,0:T(8,128)S(1)} %get-tuple-element.96.three_ref), channel_id=1, source_target_pairs={{0,16},{8,24},{16,0},{24,8},{1,17},{9,25},{17,1},{25,9},{2,18},{10... | collective-permute-start | bytes 884744 | tf_op jit(solution)/shard_map/ppermute | solution.py:21
  39.1 16.0 %collective-permute-start.9 = (f32[128,384]{1,0:T(8,128)S(1)}, f32[128,384]{1,0:T(8,128)S(1)}, u32[]{:S(2)}, u32[]{:S(2)}) collective-permute-start(f32[128,384]{1,0:T(8,128)S(1)} %collective-permute-done.5.two_c), channel_id=1, source_target_pairs={{0,16},{8,24},{16,0},{24,8},{1,17},{9,25},{17,1},{25,9},{2,18},{10... | collective-permute-start | bytes 589832 | tf_op jit(solution)/shard_map/ppermute | solution.py:21
  40.1 11.5 %collective-permute-start.7 = (f32[192,128]{1,0:T(8,128)S(1)}, f32[192,128]{1,0:T(8,128)S(1)}, u32[]{:S(2)}, u32[]{:S(2)}) collective-permute-start(f32[192,128]{1,0:T(8,128)S(1)} %get-tuple-element.100), channel_id=1, source_target_pairs={{0,4},{1,5},{2,6},{3,7},{4,0},{5,1},{6,2},{7,3},{8,12},{9,13},{10,... | collective-permute-start | bytes 294920 | tf_op jit(solution)/shard_map/ppermute | solution.py:21
  41.2 12.3 %collective-permute-start.8 = (f32[128,384]{1,0:T(8,128)S(1)}, f32[128,384]{1,0:T(8,128)S(1)}, u32[]{:S(2)}, u32[]{:S(2)}) collective-permute-start(f32[128,384]{1,0:T(8,128)S(1)} %get-tuple-element.106), channel_id=1, source_target_pairs={{0,4},{1,5},{2,6},{3,7},{4,0},{5,1},{6,2},{7,3},{8,12},{9,13},{10,... | collective-permute-start | bytes 589832 | tf_op jit(solution)/shard_map/ppermute | solution.py:21
  43.0 12.1 %collective-permute-start.10 = (f32[128,384]{1,0:T(8,128)S(1)}, f32[128,384]{1,0:T(8,128)S(1)}, u32[]{:S(2)}, u32[]{:S(2)}) collective-permute-start(f32[128,384]{1,0:T(8,128)S(1)} %collective-permute-done.4.three_c), channel_id=1, source_target_pairs={{0,16},{8,24},{16,0},{24,8},{1,17},{9,25},{17,1},{25,9},{2,18},{10... | collective-permute-start | bytes 589832 | tf_op jit(solution)/shard_map/ppermute | solution.py:21
  51.6 6.3 %collective-permute-start.12 = (f32[192,128]{1,0:T(8,128)S(1)}, f32[192,128]{1,0:T(8,128)S(1)}, u32[]{:S(2)}, u32[]{:S(2)}) collective-permute-start(f32[192,128]{1,0:T(8,128)S(1)} %add.17.total_ref), channel_id=1, source_target_pairs={{0,16},{8,24},{16,0},{24,8},{1,17},{9,25},{17,1},{25,9},{2,18},{10... | collective-permute-start | bytes 294920 | tf_op jit(solution)/shard_map/ppermute | solution.py:21
  53.5 5.7 %collective-permute-start.11 = (f32[128,384]{1,0:T(8,128)S(1)}, f32[128,384]{1,0:T(8,128)S(1)}, u32[]{:S(2)}, u32[]{:S(2)}) collective-permute-start(f32[128,384]{1,0:T(8,128)S(1)} %collective-permute-done.8.four_c), channel_id=1, source_target_pairs={{0,16},{8,24},{16,0},{24,8},{1,17},{9,25},{17,1},{25,9},{2,18},{10... | collective-permute-start | bytes 589832 | tf_op jit(solution)/shard_map/ppermute | solution.py:21
